TPU v7x, 32 devices: a whole 2x2x4 slice. The times are simulated.
32 devices in a mesh: dp: 2 (over x), row: 4 (over y, core), col: 4 (over z).
Axes of the slice: x: 2, y: 2, z: 4, core: 2. Of those that a mesh axis runs over, the one named last changes fastest.
Arguments:
- inputs: bfloat16 [8192, 1024], P(('dp', 'row'), 'col'), may hold values from -29 to 29
- query_weight: bfloat16 [1024, 1024], P('col', 'row'), may hold values from -0.1875 to 0.1875
- query_bias: float32 [1024], P('row'), may hold values from -3 to 3
- key_weight: bfloat16 [1024, 1024], P('col', 'row'), may hold values from -0.1875 to 0.1875
- value_weight: bfloat16 [1024, 1024], P('col', 'row'), may hold values from -0.1875 to 0.1875
- value_bias: float32 [1024], P('row'), may hold values from -0.3 to 0.3
- mixer_weight: bfloat16 [1024, 1024], P('row', 'col'), may hold values from -2 to 2
- mixer_bias: float32 [1024], P('col'), may hold values from -2 to 2
- norm_gain: float32 [1024], P('col'), may hold values from 0.4 to 2.3
- norm_bias: float32 [1024], P('col'), may hold values from -2 to 2
- inner_weight: bfloat16 [1024, 4096], P('col', 'row'), may hold values from -0.1875 to 0.1875
- inner_bias: float32 [4096], P('row'), may hold values from -2 to 2
- outer_weight: bfloat16 [4096, 1024], P('row', 'col'), may hold values from -0.09375 to 0.09375
- outer_bias: float32 [1024], P('col'), may hold values from -2 to 2
- final_gain: float32 [1024], P('col'), may hold values from 0.25 to 1.75
- final_bias: float32 [1024], P('col'), may hold values from -2 to 2
- cotangent: bfloat16 [8192, 1024], P(('dp', 'row'), 'col'), may hold values from -6 to 6
Outputs:
- layer_out: bfloat16 [8192, 1024], P(('dp', 'row'), 'col')
- grad_inputs: float32 [8192, 1024], P(('dp', 'row'), 'col')
- grad_queryweight: float32 [1024, 1024], P('col', 'row')
- grad_querybias: float32 [1024], P('row')
- grad_keyweight: float32 [1024, 1024], P('col', 'row')
- grad_valueweight: float32 [1024, 1024], P('col', 'row')
- grad_valuebias: float32 [1024], P('row')
- grad_mixerweight: float32 [1024, 1024], P('row', 'col')
- grad_mixerbias: float32 [1024], P('col')
- grad_normgain: float32 [1024], P('col')
- grad_normbias: float32 [1024], P('col')
- grad_innerweight: float32 [1024, 4096], P('col', 'row')
- grad_innerbias: float32 [4096], P('row')
- grad_outerweight: float32 [4096, 1024], P('row', 'col')
- grad_outerbias: float32 [1024], P('col')
- grad_finalgain: float32 [1024], P('col')
- grad_finalbias: float32 [1024], P('col')
All inputs are finite; a program needn't handle non-finite values.
Results may differ from a plain program's by a relative error of at most 0.01065.
The roundings to bfloat16 on the way count: a program that leaves them out, or rounds other values in their place, can miss the bound.
Values may be sent and summed in bfloat16 or wider, within the bound.
A program may use at most 128 MiB of HBM per device.

v0:
```python
import math

import jax
import jax.numpy as jnp
from jax import lax
from jax.sharding import PartitionSpec as P

D = 1024
DH = 64
L = 512


norm_eps = 1e-12


def multiply(left, right, flipped):
    if flipped:
        return lax.dot_general(
            left, right, (((1,), (1,)), ((), ())), preferred_element_type=jnp.float32
        )
    return jnp.dot(left, right, preferred_element_type=jnp.float32)


def outer_product(left, right):
    return lax.dot_general(
        left, right, (((0,), (0,)), ((), ())), preferred_element_type=jnp.float32
    )


def column_sums(block):
    return jnp.dot(
        jnp.ones((1, block.shape[0]), block.dtype), block, preferred_element_type=jnp.float32
    )[0]


def rows_gather(block):
    return lax.all_gather(block, "row", axis=0, tiled=True)


def cols_gather(block):
    return lax.all_gather(block, "col", axis=0, tiled=True)


def row_reduce(gathered, weight, flipped):
    return lax.psum_scatter(
        multiply(gathered, weight, flipped), "row", scatter_dimension=0, tiled=True
    )


def col_partial(gathered, weight, flipped):
    return lax.psum_scatter(
        multiply(gathered, weight, flipped), "col", scatter_dimension=0, tiled=True
    )


def col_reduce(gathered, weight):
    return col_partial(gathered, weight, True)


def column_product(gathered, weight):
    return col_partial(gathered, weight, False)


def stats_sum(first, second):
    return lax.psum((first, second), "col")


def normalize(total):
    first, second = stats_sum(jnp.sum(total, axis=-1), jnp.sum(total * total, axis=-1))
    center = first / D
    spread = second / D - center * center
    scale = lax.rsqrt(spread + norm_eps)
    return ((total - center[:, None]) * scale[:, None], scale)


def norm_back(scaled_grad, normed, scale):
    first, second = stats_sum(jnp.sum(scaled_grad, axis=-1), jnp.sum(scaled_grad * normed, axis=-1))
    return scale[:, None] * (scaled_grad - first[:, None] / D - normed * (second[:, None] / D))


def gelu_slope(values):
    normal_cdf = 0.5 * (1.0 + jax.scipy.special.erf(values * (1.0 / math.sqrt(2.0))))
    density = jnp.exp(-0.5 * values * values) * (1.0 / math.sqrt(2.0 * math.pi))
    return normal_cdf + values * density


def split_heads(block, heads):
    return block.reshape(-1, L, heads, DH)


def attend(query_rows, key_rows, value_rows, heads):
    factor = DH ** (-0.5)
    scores = (
        jnp.einsum(
            "bqhd,bkhd->bhqk",
            split_heads(query_rows, heads),
            split_heads(key_rows, heads),
            preferred_element_type=jnp.float32,
        )
        * factor
    )
    top = jnp.max(scores, axis=-1, keepdims=True)
    weights = jnp.exp(scores - top)
    total = jnp.sum(weights, axis=-1, keepdims=True)
    low_probs = (weights / total).astype(jnp.bfloat16)
    context = jnp.einsum(
        "bhqk,bkhd->bqhd",
        low_probs,
        split_heads(value_rows, heads),
        preferred_element_type=jnp.float32,
    )
    return (context.reshape(query_rows.shape[0], -1).astype(jnp.bfloat16), top + jnp.log(total))


def attend_back(query_rows, key_rows, value_rows, log_total, context_grad, heads):
    factor = DH ** (-0.5)
    query_heads = split_heads(query_rows, heads)
    key_heads = split_heads(key_rows, heads)
    value_heads = split_heads(value_rows, heads)
    grad_heads = split_heads(context_grad, heads)
    scores = (
        jnp.einsum("bqhd,bkhd->bhqk", query_heads, key_heads, preferred_element_type=jnp.float32)
        * factor
    )
    probs = jnp.exp(scores - log_total)
    low_probs = probs.astype(jnp.bfloat16)
    value_grad = jnp.einsum(
        "bhqk,bqhd->bkhd", low_probs, grad_heads, preferred_element_type=jnp.float32
    )
    prob_grad = jnp.einsum(
        "bqhd,bkhd->bhqk", grad_heads, value_heads, preferred_element_type=jnp.float32
    )
    inner_sum = jnp.sum(probs * prob_grad, axis=-1, keepdims=True)
    score_grad = (probs * (prob_grad - inner_sum)).astype(jnp.bfloat16)
    query_grad = (
        jnp.einsum("bhqk,bkhd->bqhd", score_grad, key_heads, preferred_element_type=jnp.float32)
        * factor
    )
    key_grad = (
        jnp.einsum("bhqk,bqhd->bkhd", score_grad, query_heads, preferred_element_type=jnp.float32)
        * factor
    )
    count = query_rows.shape[0]
    joined = jnp.concatenate(
        [query_grad.reshape(count, -1), key_grad.reshape(count, -1), value_grad.reshape(count, -1)],
        axis=1,
    )
    return joined.astype(jnp.bfloat16)


def local(
    inputs,
    query_weight,
    query_bias,
    key_weight,
    value_weight,
    value_bias,
    mixer_weight,
    mixer_bias,
    norm_gain,
    norm_bias,
    inner_weight,
    inner_bias,
    outer_weight,
    outer_bias,
    final_gain,
    final_bias,
    cotangent,
):
    head_width = query_weight.shape[1]
    heads = head_width // DH
    joint_weight = jnp.concatenate([query_weight, key_weight, value_weight], axis=1)
    gathered_in = rows_gather(inputs)
    projected = column_product(gathered_in, joint_weight)
    query_rows = (projected[:, :head_width] + query_bias).astype(jnp.bfloat16)
    key_rows = projected[:, head_width : 2 * head_width].astype(jnp.bfloat16)
    value_rows = (projected[:, 2 * head_width :] + value_bias).astype(jnp.bfloat16)
    context, log_total = attend(query_rows, key_rows, value_rows, heads)
    gathered_ctx = cols_gather(context)
    mixed = row_reduce(gathered_ctx, mixer_weight, False)
    first_sum = inputs.astype(jnp.float32) + mixed + mixer_bias
    first_hat, first_scale = normalize(first_sum)
    first_out = first_hat * norm_gain + norm_bias
    gathered_mid = rows_gather(first_out.astype(jnp.bfloat16))
    inner_pre = column_product(gathered_mid, inner_weight) + inner_bias
    activated = jax.nn.gelu(inner_pre, approximate=False).astype(jnp.bfloat16)
    gathered_act = cols_gather(activated)
    outer = row_reduce(gathered_act, outer_weight, False)
    second_sum = first_out + outer + outer_bias
    second_hat, second_scale = normalize(second_sum)
    layer_out = (second_hat * final_gain + final_bias).astype(jnp.bfloat16)
    upstream = cotangent.astype(jnp.float32)
    grad_finalgain = jnp.sum(upstream * second_hat, axis=0)
    grad_finalbias = jnp.sum(upstream, axis=0)
    second_grad = norm_back(upstream * final_gain, second_hat, second_scale)
    second_low = second_grad.astype(jnp.bfloat16)
    grad_outerbias = column_sums(second_low)
    gathered_second = rows_gather(second_low)
    act_grad = col_reduce(gathered_second, outer_weight)
    grad_outerweight = outer_product(gathered_act, gathered_second)
    inner_grad = (act_grad * gelu_slope(inner_pre)).astype(jnp.bfloat16)
    gathered_inner = cols_gather(inner_grad)
    grad_innerbias = column_sums(gathered_inner)
    mid_grad = row_reduce(gathered_inner, inner_weight, True)
    grad_innerweight = outer_product(gathered_mid, gathered_inner)
    first_up = second_grad + mid_grad
    grad_normgain = jnp.sum(first_up * first_hat, axis=0)
    grad_normbias = jnp.sum(first_up, axis=0)
    first_grad = norm_back(first_up * norm_gain, first_hat, first_scale)
    first_low = first_grad.astype(jnp.bfloat16)
    grad_mixerbias = column_sums(first_low)
    gathered_first = rows_gather(first_low)
    context_grad = col_reduce(gathered_first, mixer_weight).astype(jnp.bfloat16)
    grad_mixerweight = outer_product(gathered_ctx, gathered_first)
    joint_grad = attend_back(query_rows, key_rows, value_rows, log_total, context_grad, heads)
    gathered_joint = cols_gather(joint_grad)
    joint_bias = column_sums(gathered_joint)
    input_part = row_reduce(gathered_joint, joint_weight, True)
    grad_joint = outer_product(gathered_in, gathered_joint)
    grad_inputs = first_grad + input_part
    grad_outerweight, grad_innerweight, grad_innerbias, grad_mixerweight, grad_joint, joint_bias = (
        lax.psum(
            (
                grad_outerweight,
                grad_innerweight,
                grad_innerbias,
                grad_mixerweight,
                grad_joint,
                joint_bias,
            ),
            "dp",
        )
    )
    grad_normgain, grad_normbias, grad_finalgain, grad_finalbias, grad_mixerbias, grad_outerbias = (
        lax.psum(
            (
                grad_normgain,
                grad_normbias,
                grad_finalgain,
                grad_finalbias,
                grad_mixerbias,
                grad_outerbias,
            ),
            ("dp", "row"),
        )
    )
    grad_queryweight = grad_joint[:, :head_width]
    grad_keyweight = grad_joint[:, head_width : 2 * head_width]
    grad_valueweight = grad_joint[:, 2 * head_width :]
    grad_querybias = joint_bias[:head_width]
    grad_valuebias = joint_bias[2 * head_width :]
    return (
        layer_out,
        grad_inputs,
        grad_queryweight,
        grad_querybias,
        grad_keyweight,
        grad_valueweight,
        grad_valuebias,
        grad_mixerweight,
        grad_mixerbias,
        grad_normgain,
        grad_normbias,
        grad_innerweight,
        grad_innerbias,
        grad_outerweight,
        grad_outerbias,
        grad_finalgain,
        grad_finalbias,
    )


def solution(mesh):
    return jax.shard_map(
        local,
        mesh=mesh,
        in_specs=(
            P(("dp", "row"), "col"),
            P("col", "row"),
            P("row"),
            P("col", "row"),
            P("col", "row"),
            P("row"),
            P("row", "col"),
            P("col"),
            P("col"),
            P("col"),
            P("col", "row"),
            P("row"),
            P("row", "col"),
            P("col"),
            P("col"),
            P("col"),
            P(("dp", "row"), "col"),
        ),
        out_specs=(
            P(("dp", "row"), "col"),
            P(("dp", "row"), "col"),
            P("col", "row"),
            P("row"),
            P("col", "row"),
            P("col", "row"),
            P("row"),
            P("row", "col"),
            P("col"),
            P("col"),
            P("col"),
            P("col", "row"),
            P("row"),
            P("row", "col"),
            P("col"),
            P("col"),
            P("col"),
        ),
        check_vma=False,
    )
```

profile of v0, /device:TPU:24, one launch (start us, length us, event | category | flops | bytes accessed | tf_op | source)
XLA Modules:
  0.0 1855.1 jit_solution(16413659531410080877)
XLA Ops:
  9.8 0.9 constant_dynamic-update-slice_fusion
  10.7 22.5 %all-gather.9.cloned.1.call-done = bf16[4096,256]{1,0:T(8,128)(2,1)} async-done(((bf16[1024,256]{1,0:T(8,128)(2,1)}), bf16[4096,256]{1,0:T(8,128)(2,1)}) %all-gather.9.cloned.1.call-update) | async-done | bytes 2097168 | tf_op jit(solution)/shard_map/all_gather | solution.py:37
  33.2 8.0 convolution_bitcast_fusion
  41.3 211.7 %reduce-scatter.9.cloned.1.call-done = f32[1024,768]{0,1:T(8,128)} async-done(((f32[4096,768]{0,1:T(8,128)}), f32[1024,768]{0,1:T(8,128)}) %reduce-scatter.9.cloned.1.call-update) | async-done | bytes 3145744 | tf_op jit(solution)/shard_map/reduce_scatter | solution.py:51
  253.0 1.3 slice.46
  254.7 1.7 fusion.43
  257.2 1.3 multiply_reduce_fusion.1
  258.5 1.4 fusion
  260.0 1.8 copy-done.2
  261.8 1.9 fusion.37
  265.2 45.1 %all-gather.11.cloned.1.call-done = bf16[4096,256]{0,1:T(8,128)(2,1)} async-done(((bf16[1024,256]{0,1:T(8,128)(2,1)}), bf16[4096,256]{0,1:T(8,128)(2,1)}) %all-gather.11.cloned.1.call-update) | async-done | bytes 2097168 | tf_op jit(solution)/shard_map/all_gather | solution.py:41
  310.3 4.3 fusion.74
  314.7 45.5 %reduce-scatter.11.cloned.1.call-done = f32[1024,256]{1,0:T(8,128)} async-done(((f32[4096,256]{1,0:T(8,128)}), f32[1024,256]{1,0:T(8,128)}) %reduce-scatter.11.cloned.1.call-update) | async-done | bytes 1048592 | tf_op jit(solution)/shard_map/reduce_scatter | solution.py:45
  360.2 2.2 fusion.69
  362.4 8.4 all-reduce.4
  370.8 1.8 fusion.44
  372.9 23.4 %all-gather.13.cloned.1.call-done = bf16[4096,256]{1,0:T(8,128)(2,1)} async-done(((bf16[1024,256]{1,0:T(8,128)(2,1)}), bf16[4096,256]{1,0:T(8,128)(2,1)}) %all-gather.13.cloned.1.call-update) | async-done | bytes 2097168 | tf_op jit(solution)/shard_map/all_gather | solution.py:37
  396.3 9.7 fusion.75
  406.0 279.9 %reduce-scatter.13.cloned.1.call-done = f32[1024,1024]{1,0:T(8,128)} async-done(((f32[4096,1024]{1,0:T(8,128)}), f32[1024,1024]{1,0:T(8,128)}) %reduce-scatter.13.cloned.1.call-update) | async-done | bytes 4194320 | tf_op jit(solution)/shard_map/reduce_scatter | solution.py:51
  686.0 11.4 fusion.6
  697.4 147.9 %all-gather.15.cloned.1.call-done = bf16[4096,1024]{1,0:T(8,128)(2,1)} async-done(((bf16[1024,1024]{1,0:T(8,128)(2,1)}), bf16[4096,1024]{1,0:T(8,128)(2,1)}) %all-gather.15.cloned.1.call-update) | async-done | bytes 8388624 | tf_op jit(solution)/shard_map/all_gather | solution.py:41
  845.3 7.7 fusion.76
  853.1 45.9 %reduce-scatter.15.cloned.1.call-done = f32[1024,256]{1,0:T(8,128)} async-done(((f32[4096,256]{1,0:T(8,128)}), f32[1024,256]{1,0:T(8,128)}) %reduce-scatter.15.cloned.1.call-update) | async-done | bytes 1048592 | tf_op jit(solution)/shard_map/reduce_scatter | solution.py:45
  898.9 2.5 fusion.68
  901.4 8.9 all-reduce.3
  911.7 2.3 fusion.41
  914.0 11.5 all-reduce.2
  926.8 2.8 fusion.67
  929.6 22.7 %all-gather.17.cloned.1.call-done = bf16[4096,256]{1,0:T(8,128)(2,1)} async-done(((bf16[1024,256]{1,0:T(8,128)(2,1)}), bf16[4096,256]{1,0:T(8,128)(2,1)}) %all-gather.17.cloned.1.call-update) | async-done | bytes 2097168 | tf_op jit(solution)/shard_map/all_gather | solution.py:37
  952.3 9.7 fusion.77
  962.5 279.5 %reduce-scatter.17.cloned.1.call-done = f32[1024,1024]{1,0:T(8,128)} async-done(((f32[4096,1024]{1,0:T(8,128)}), f32[1024,1024]{1,0:T(8,128)}) %reduce-scatter.17.cloned.1.call-update) | async-done | bytes 4194320 | tf_op jit(solution)/shard_map/reduce_scatter | solution.py:51
  1242.0 5.4 fusion.12
  1247.5 147.9 %all-gather.19.cloned.1.call-done = bf16[4096,1024]{1,0:T(8,128)(2,1)} async-done(((bf16[1024,1024]{1,0:T(8,128)(2,1)}), bf16[4096,1024]{1,0:T(8,128)(2,1)}) %all-gather.19.cloned.1.call-update) | async-done | bytes 8388624 | tf_op jit(solution)/shard_map/all_gather | solution.py:41
  1395.5 7.7 fusion.78
  1403.3 45.9 %reduce-scatter.19.cloned.1.call-done = f32[1024,256]{1,0:T(8,128)} async-done(((f32[4096,256]{1,0:T(8,128)}), f32[1024,256]{1,0:T(8,128)}) %reduce-scatter.19.cloned.1.call-update) | async-done | bytes 1048592 | tf_op jit(solution)/shard_map/reduce_scatter | solution.py:45
  1449.1 3.9 multiply_reduce_fusion.2
  1453.0 8.4 all-reduce.1
  1461.4 3.1 fusion.70
  1464.6 23.6 %all-gather.21.cloned.1.call-done = bf16[4096,256]{1,0:T(8,128)(2,1)} async-done(((bf16[1024,256]{1,0:T(8,128)(2,1)}), bf16[4096,256]{1,0:T(8,128)(2,1)}) %all-gather.21.cloned.1.call-update) | async-done | bytes 2097168 | tf_op jit(solution)/shard_map/all_gather | solution.py:37
  1488.2 4.3 fusion.79
  1493.2 75.5 %reduce-scatter.21.cloned.1.call-done = f32[1024,256]{1,0:T(8,128)} async-done(((f32[4096,256]{1,0:T(8,128)}), f32[1024,256]{1,0:T(8,128)}) %reduce-scatter.21.cloned.1.call-update) | async-done | bytes 1048592 | tf_op jit(solution)/shard_map/reduce_scatter | solution.py:51
  1568.6 1.3 convert_element_type.67
  1571.0 5.1 fusion.34
  1576.1 4.8 multiply_reduce_fusion
  1580.9 2.5 multiply_convert_fusion
  1583.4 1.4 fusion.32
  1587.5 1.3 pad_maximum_fusion
  1589.0 7.4 fusion.83
  1596.4 7.8 fusion.82
  1604.2 1.4 fusion.81
  1605.6 96.9 %all-gather.23.cloned.1.call-done = bf16[4096,768]{0,1:T(8,128)(2,1)} async-done(((bf16[1024,768]{0,1:T(8,128)(2,1)}), bf16[4096,768]{0,1:T(8,128)(2,1)}) %all-gather.23.cloned.1.call-update) | async-done | bytes 6291472 | tf_op jit(solution)/shard_map/all_gather | solution.py:41
  1702.5 5.5 convolution_bitcast_fusion.1
  1708.1 6.6 fusion.80
  1714.7 1.2 copy-done.9
  1716.1 4.7 fusion.53
  1721.0 15.4 all-reduce
  1736.4 4.6 convolution_reduce_fusion
  1741.0 5.7 all-reduce.5
  1747.4 48.9 %all-reduce.9.cloned.1.call-done = (f32[256,768]{0,1:T(8,128)}, f32[256,256]{1,0:T(8,128)}, f32[256,1024]{1,0:T(8,128)}, f32[1024,256]{1,0:T(8,128)}) async-done(((f32[256,768]{0,1:T(8,128)}, f32[256,256]{1,0:T(8,128)}, f32[256,1024]{1,0:T(8,128)}, f32[1024,256]{1,0:T(8,128)}), (f32[256,768]{0,1:T(8,128)}, f32[256,256]{1,0:T(8,128)}, f32[256,1024]{1,0:T(8,128)}, ...) | async-done | bytes 3145744 | tf_op jit(solution)/shard_map/psum | solution.py:222
  1796.2 1.3 fusion.72
  1800.0 43.3 %reduce-scatter.23.cloned.1.call-done = f32[1024,256]{1,0:T(8,128)} async-done(((f32[4096,256]{1,0:T(8,128)}), f32[1024,256]{1,0:T(8,128)}) %reduce-scatter.23.cloned.1.call-update) | async-done | bytes 1048592 | tf_op jit(solution)/shard_map/reduce_scatter | solution.py:45
  1843.3 2.4 add.166
  1846.4 1.0 copy.104
  1847.4 1.0 copy.105
  (142 shorter events, 18.0 us)
Async XLA Ops:
  7.2 838.1 %copy-start = (bf16[1024,256]{1,0:T(8,128)(2,1)S(1)}, bf16[1024,256]{1,0:T(8,128)(2,1)}, u32[]{:S(2)}) copy-start(bf16[1024,256]{1,0:T(8,128)(2,1)} %param.29) | copy-start | bytes 1572868
  7.2 26.0 %all-gather.9.cloned.1.call-start = ((), (), s32[]{:S(2)}) async-start(), calls=%async_computation.8 | async-start | bytes 2621440 | tf_op jit(solution)/shard_map/all_gather | solution.py:37
  7.9 245.0 %reduce-scatter.9.cloned.1.call-start = ((), (), s32[]{:S(2)}) async-start(), calls=%async_computation.9 | async-start | bytes 15728640 | tf_op jit(solution)/shard_map/reduce_scatter | solution.py:51
  41.2 213.5 %copy-start.36 = (f32[256]{0:T(256)S(1)}, f32[256]{0:T(256)}, u32[]{:S(2)}) copy-start(f32[256]{0:T(256)} %param.22) | copy-start | bytes 3076
  41.2 213.5 %copy-start.37 = (f32[256]{0:T(256)S(1)}, f32[256]{0:T(256)}, u32[]{:S(2)}) copy-start(f32[256]{0:T(256)} %param.19) | copy-start | bytes 3076
  41.2 269.1 %all-gather.11.cloned.1.call-start = ((), (), s32[]{:S(2)}) async-start(), calls=%async_computation.10 | async-start | bytes 2621440 | tf_op jit(solution)/shard_map/all_gather | solution.py:41
  256.8 3.2 copy-start.14
  257.2 1.3 copy-start.6
  258.5 3.2 copy-start.2
  261.8 1.9 copy-start.27
  261.8 48.5 %copy-start.18 = (bf16[256,256]{1,0:T(8,128)(2,1)S(1)}, bf16[256,256]{1,0:T(8,128)(2,1)}, u32[]{:S(2)}) copy-start(bf16[256,256]{1,0:T(8,128)(2,1)} %param.23) | copy-start | bytes 393220
  265.1 95.1 %reduce-scatter.11.cloned.1.call-start = ((), (), s32[]{:S(2)}) async-start(), calls=%async_computation.11 | async-start | bytes 5242880 | tf_op jit(solution)/shard_map/reduce_scatter | solution.py:45
  314.6 45.6 %copy-start.13 = (bf16[1024,256]{1,0:T(8,128)(2,1)S(1)}, bf16[1024,256]{1,0:T(8,128)(2,1)}, u32[]{:S(2)}) copy-start(bf16[1024,256]{1,0:T(8,128)(2,1)} %param.17) | copy-start | bytes 1572868
  314.6 81.7 %copy-start.20 = (bf16[256,1024]{1,0:T(8,128)(2,1)S(1)}, bf16[256,1024]{1,0:T(8,128)(2,1)}, u32[]{:S(2)}) copy-start(bf16[256,1024]{1,0:T(8,128)(2,1)} %param.27) | copy-start | bytes 1572868
  314.6 81.6 %all-gather.13.cloned.1.call-start = ((), (), s32[]{:S(2)}) async-start(), calls=%async_computation.12 | async-start | bytes 2621440 | tf_op jit(solution)/shard_map/all_gather | solution.py:37
  370.8 35.1 %copy-start.23 = (f32[1024]{0:T(1024)}, f32[1024]{0:T(1024)S(1)}, u32[]{:S(2)}) copy-start(f32[1024]{0:T(1024)S(1)} %get-tuple-element.98) | copy-start | bytes 12292
  370.8 35.1 %copy-start.24 = (f32[1024]{0:T(1024)}, f32[1024]{0:T(1024)S(1)}, u32[]{:S(2)}) copy-start(f32[1024]{0:T(1024)S(1)} %get-tuple-element.99) | copy-start | bytes 12292
  372.7 313.3 %reduce-scatter.13.cloned.1.call-start = ((), (), s32[]{:S(2)}) async-start(), calls=%async_computation.13 | async-start | bytes 20971520 | tf_op jit(solution)/shard_map/reduce_scatter | solution.py:51
  406.0 280.0 %copy-start.31 = (f32[1024]{0:T(1024)S(1)}, f32[1024]{0:T(1024)}, u32[]{:S(2)}) copy-start(f32[1024]{0:T(1024)} %param.28) | copy-start | bytes 12292
  406.0 439.3 %all-gather.15.cloned.1.call-start = ((), (), s32[]{:S(2)}) async-start(), calls=%async_computation.14 | async-start | bytes 10485760 | tf_op jit(solution)/shard_map/all_gather | solution.py:41
  697.3 201.6 %reduce-scatter.15.cloned.1.call-start = ((), (), s32[]{:S(2)}) async-start(), calls=%async_computation.15 | async-start | bytes 5242880 | tf_op jit(solution)/shard_map/reduce_scatter | solution.py:45
  853.0 99.3 %all-gather.17.cloned.1.call-start = ((), (), s32[]{:S(2)}) async-start(), calls=%async_computation.16 | async-start | bytes 2621440 | tf_op jit(solution)/shard_map/all_gather | solution.py:37
  911.1 0.6 copy-start.25
  911.1 2.9 copy-start.26
  926.2 0.6 copy-start.29
  926.2 0.6 copy-start.30
  929.6 312.5 %reduce-scatter.17.cloned.1.call-start = ((), (), s32[]{:S(2)}) async-start(), calls=%async_computation.17 | async-start | bytes 20971520 | tf_op jit(solution)/shard_map/reduce_scatter | solution.py:51
  962.1 433.4 %copy-start.21 = (bf16[256,1024]{1,0:T(8,128)(2,1)S(1)}, bf16[256,1024]{1,0:T(8,128)(2,1)}, u32[]{:S(2)}) copy-start(bf16[256,1024]{1,0:T(8,128)(2,1)} %param.27) | copy-start | bytes 1572868
  962.1 433.4 %all-gather.19.cloned.1.call-start = ((), (), s32[]{:S(2)}) async-start(), calls=%async_computation.18 | async-start | bytes 10485760 | tf_op jit(solution)/shard_map/all_gather | solution.py:41
  1247.5 201.7 %reduce-scatter.19.cloned.1.call-start = ((), (), s32[]{:S(2)}) async-start(), calls=%async_computation.19 | async-start | bytes 5242880 | tf_op jit(solution)/shard_map/reduce_scatter | solution.py:45
  1403.2 45.9 %copy-start.8 = (bf16[1024,256]{1,0:T(8,128)(2,1)S(1)}, bf16[1024,256]{1,0:T(8,128)(2,1)}, u32[]{:S(2)}) copy-start(bf16[1024,256]{1,0:T(8,128)(2,1)} %param.33) | copy-start | bytes 1572868
  1403.2 84.9 %all-gather.21.cloned.1.call-start = ((), (), s32[]{:S(2)}) async-start(), calls=%async_computation.20 | async-start | bytes 2621440 | tf_op jit(solution)/shard_map/all_gather | solution.py:37
  1453.0 35.1 %copy-start.19 = (bf16[256,256]{1,0:T(8,128)(2,1)S(1)}, bf16[256,256]{1,0:T(8,128)(2,1)}, u32[]{:S(2)}) copy-start(bf16[256,256]{1,0:T(8,128)(2,1)} %param.23) | copy-start | bytes 393220
  1464.5 104.1 %reduce-scatter.21.cloned.1.call-start = ((), (), s32[]{:S(2)}) async-start(), calls=%async_computation.21 | async-start | bytes 5242880 | tf_op jit(solution)/shard_map/reduce_scatter | solution.py:51
  1492.5 0.7 copy-start.28
  1492.5 210.0 %all-gather.23.cloned.1.call-start = ((), (), s32[]{:S(2)}) async-start(), calls=%async_computation.22 | async-start | bytes 7864320 | tf_op jit(solution)/shard_map/all_gather | solution.py:41
  1571.0 5.1 copy-start.15
  1571.0 9.9 slice-start
  1576.1 4.8 slice-start.1
  1580.9 2.5 copy-start.7
  1588.8 7.7 copy-start.4
  1588.8 207.4 %all-reduce.9.cloned.1.call-start = ((), (), s32[]{:S(2)}) async-start(), calls=%async_computation.24 | async-start | bytes 6291456 | tf_op jit(solution)/shard_map/psum | solution.py:222
  1596.4 7.8 copy-start.3
  1596.4 7.8 copy-start.5
  1604.2 98.3 %copy-start.12 = (bf16[4096,256]{1,0:T(8,128)(2,1)S(1)}, bf16[4096,256]{1,0:T(8,128)(2,1)}, u32[]{:S(2)}) copy-start(bf16[4096,256]{1,0:T(8,128)(2,1)} %all-gather.9.cloned.1.call-done) | copy-start | bytes 6291460
  1708.0 135.3 %reduce-scatter.23.cloned.1.call-start = ((), (), s32[]{:S(2)}) async-start(), calls=%async_computation.23 | async-start | bytes 5242880 | tf_op jit(solution)/shard_map/reduce_scatter | solution.py:45
  1714.7 1.2 copy-start.9
  1716.0 4.8 copy-start.10
  1716.0 4.9 copy-start.32
  1716.1 4.9 copy-start.33
  1716.1 4.9 copy-start.34
  1716.1 4.9 copy-start.35
  1736.4 106.9 %copy-start.11 = (f32[1024,256]{1,0:T(8,128)S(1)}, f32[1024,256]{1,0:T(8,128)}, u32[]{:S(2)}) copy-start(f32[1024,256]{1,0:T(8,128)} %get-tuple-element.84) | copy-start | bytes 3145732
  1796.2 49.5 %copy-start.22 = (f32[256,256]{1,0:T(8,128)S(1)}, f32[256,256]{1,0:T(8,128)}, u32[]{:S(2)}) copy-start(f32[256,256]{1,0:T(8,128)} %get-tuple-element.113) | copy-start | bytes 786436
  1796.2 51.2 %copy-start.16 = (f32[1024,256]{1,0:T(8,128)S(1)}, f32[1024,256]{1,0:T(8,128)}, u32[]{:S(2)}) copy-start(f32[1024,256]{1,0:T(8,128)} %get-tuple-element.119) | copy-start | bytes 3145732
  1799.2 49.2 %copy-start.1 = (bf16[1024,256]{1,0:T(8,128)(2,1)S(1)}, bf16[1024,256]{1,0:T(8,128)(2,1)}, u32[]{:S(2)}) copy-start(bf16[1024,256]{1,0:T(8,128)(2,1)} %param.29) | copy-start | bytes 1572868
  1843.3 3.1 copy-start.17
Sparse Core Ops, SparseCore 0:
  9.6 23.5 all-gather.8
  41.3 211.6 reduce-scatter.8
  265.2 45.0 all-gather.10
  314.8 45.4 reduce-scatter.10
  372.8 23.4 all-gather.12
  406.1 279.8 reduce-scatter.12
  697.5 147.8 all-gather.14
  853.1 45.7 reduce-scatter.14
  929.7 22.6 all-gather.16
  962.2 279.8 reduce-scatter.16
  1247.6 147.8 all-gather.18
  1403.3 45.7 reduce-scatter.18
  1464.7 23.4 all-gather.20
  1492.6 75.9 reduce-scatter.20
  1588.9 113.5 all-gather.22
  1708.1 88.0 all-reduce.8
  1798.8 44.5 reduce-scatter.22
where the time goes:
time: 1860 us
  waiting for transfers between devices  1610 us (87%)
  matrix products  105 us (6%)
  blocking collectives  58.3 us (3%)
  other arithmetic  47.4 us (3%)
  local copies, waits for them, and re-layouts  21.4 us (1%)
    reduce_scatter x4, waiting for transfers between devices, col_partial(): lax.psum_scatter(multiply(gathered, weight, flipped), 'col', scatter_dime...  847 us
    all_gather x4, waiting for transfers between devices, cols_gather(): return lax.all_gather(block, 'col', axis=0, tiled=True)  438 us
    reduce_scatter x4, waiting for transfers between devices, row_reduce(): lax.psum_scatter(multiply(gathered, weight, flipped), 'row', scatter_dime...  181 us
    all_gather x4, waiting for transfers between devices, rows_gather(): return lax.all_gather(block, 'row', axis=0, tiled=True)  92.1 us
    psum x1, waiting for transfers between devices, local(): lax.psum((grad_outerweight, grad_innerweight, grad_innerbias, grad_mixerw...  48.9 us
  transfers between devices with their start and end apart: 17, of which 17 were waited for; matrix products, arithmetic and copies ran while one was open for 2% of the time, Pallas kernels for 0%

commit v1 on v0

--- a/solution.py
+++ b/solution.py
@@ -41,41 +41,38 @@
     return lax.all_gather(block, "col", axis=0, tiled=True)
 
 
-def row_reduce(gathered, weight, flipped):
+def transposed(block):
+    row_count, col_count = lax.axis_size("row"), lax.axis_size("col")
+    pairs = [
+        (r * col_count + c, c * col_count + r) for r in range(row_count) for c in range(col_count)
+    ]
+    return lax.ppermute(block, ("row", "col"), pairs)
+
+
+def row_reduce(partial, dimension=0):
     return lax.psum_scatter(
-        multiply(gathered, weight, flipped), "row", scatter_dimension=0, tiled=True
-    )
-
-
-def col_partial(gathered, weight, flipped):
-    return lax.psum_scatter(
-        multiply(gathered, weight, flipped), "col", scatter_dimension=0, tiled=True
-    )
-
-
-def col_reduce(gathered, weight):
-    return col_partial(gathered, weight, True)
-
-
-def column_product(gathered, weight):
-    return col_partial(gathered, weight, False)
-
-
-def stats_sum(first, second):
-    return lax.psum((first, second), "col")
+        partial.astype(jnp.bfloat16), "row", scatter_dimension=dimension, tiled=True
+    )
+
+
+def grad_reduce(partial):
+    scattered = lax.psum_scatter(
+        partial.astype(jnp.bfloat16), "col", scatter_dimension=0, tiled=True
+    )
+    return lax.psum(scattered, "dp").astype(jnp.float32)
 
 
 def normalize(total):
-    first, second = stats_sum(jnp.sum(total, axis=-1), jnp.sum(total * total, axis=-1))
-    center = first / D
-    spread = second / D - center * center
-    scale = lax.rsqrt(spread + norm_eps)
-    return ((total - center[:, None]) * scale[:, None], scale)
+    center = jnp.mean(total, axis=-1, keepdims=True)
+    moved = total - center
+    scale = lax.rsqrt(jnp.mean(moved * moved, axis=-1, keepdims=True) + norm_eps)
+    return moved * scale, scale
 
 
 def norm_back(scaled_grad, normed, scale):
-    first, second = stats_sum(jnp.sum(scaled_grad, axis=-1), jnp.sum(scaled_grad * normed, axis=-1))
-    return scale[:, None] * (scaled_grad - first[:, None] / D - normed * (second[:, None] / D))
+    first = jnp.mean(scaled_grad, axis=-1, keepdims=True)
+    second = jnp.mean(scaled_grad * normed, axis=-1, keepdims=True)
+    return scale * (scaled_grad - first - normed * second)
 
 
 def gelu_slope(values):
@@ -169,80 +166,101 @@
 ):
     head_width = query_weight.shape[1]
     heads = head_width // DH
-    joint_weight = jnp.concatenate([query_weight, key_weight, value_weight], axis=1)
-    gathered_in = rows_gather(inputs)
-    projected = column_product(gathered_in, joint_weight)
+    row_at, col_at = lax.axis_index("row"), lax.axis_index("col")
+    chunk = inputs.shape[0] // lax.axis_size("row")
+    width = inputs.shape[1]
+
+    input_all = lax.all_gather(transposed(inputs), "row", axis=1, tiled=True)
+    attention_weights = cols_gather(
+        jnp.concatenate([query_weight, key_weight, value_weight, mixer_weight.T], axis=1)
+    )
+    joint_weight = attention_weights[:, : 3 * head_width]
+    mixer_turned = attention_weights[:, 3 * head_width :]
+    inner_full = cols_gather(inner_weight)
+    outer_turned = cols_gather(outer_weight.T)
+    vectors = lax.all_gather(
+        jnp.stack([mixer_bias, norm_gain, norm_bias, outer_bias, final_gain, final_bias]),
+        "col",
+        axis=1,
+        tiled=True,
+    )
+    mixer_bias, norm_gain, norm_bias, outer_bias, final_gain, final_bias = (
+        vectors[i] for i in range(6)
+    )
+    upstream = lax.all_to_all(
+        transposed(cotangent), "row", split_axis=0, concat_axis=1, tiled=True
+    ).astype(jnp.float32)
+
+    input_own = lax.dynamic_slice_in_dim(input_all, row_at * chunk, chunk, axis=0)
+    projected = multiply(input_all, joint_weight, False)
     query_rows = (projected[:, :head_width] + query_bias).astype(jnp.bfloat16)
     key_rows = projected[:, head_width : 2 * head_width].astype(jnp.bfloat16)
     value_rows = (projected[:, 2 * head_width :] + value_bias).astype(jnp.bfloat16)
     context, log_total = attend(query_rows, key_rows, value_rows, heads)
-    gathered_ctx = cols_gather(context)
-    mixed = row_reduce(gathered_ctx, mixer_weight, False)
-    first_sum = inputs.astype(jnp.float32) + mixed + mixer_bias
+    mixed = row_reduce(multiply(context, mixer_turned, True)).astype(jnp.float32)
+    first_sum = input_own.astype(jnp.float32) + mixed + mixer_bias
     first_hat, first_scale = normalize(first_sum)
     first_out = first_hat * norm_gain + norm_bias
-    gathered_mid = rows_gather(first_out.astype(jnp.bfloat16))
-    inner_pre = column_product(gathered_mid, inner_weight) + inner_bias
+    mid_all = rows_gather(first_out.astype(jnp.bfloat16))
+    inner_pre = multiply(mid_all, inner_full, False) + inner_bias
     activated = jax.nn.gelu(inner_pre, approximate=False).astype(jnp.bfloat16)
-    gathered_act = cols_gather(activated)
-    outer = row_reduce(gathered_act, outer_weight, False)
+    outer = row_reduce(multiply(activated, outer_turned, True)).astype(jnp.float32)
     second_sum = first_out + outer + outer_bias
     second_hat, second_scale = normalize(second_sum)
-    layer_out = (second_hat * final_gain + final_bias).astype(jnp.bfloat16)
-    upstream = cotangent.astype(jnp.float32)
+    layer_rows = (second_hat * final_gain + final_bias).astype(jnp.bfloat16)
+    layer_out = transposed(
+        lax.all_to_all(layer_rows, "row", split_axis=1, concat_axis=0, tiled=True)
+    )
     grad_finalgain = jnp.sum(upstream * second_hat, axis=0)
     grad_finalbias = jnp.sum(upstream, axis=0)
     second_grad = norm_back(upstream * final_gain, second_hat, second_scale)
     second_low = second_grad.astype(jnp.bfloat16)
     grad_outerbias = column_sums(second_low)
-    gathered_second = rows_gather(second_low)
-    act_grad = col_reduce(gathered_second, outer_weight)
-    grad_outerweight = outer_product(gathered_act, gathered_second)
+    second_all = rows_gather(second_low)
+    act_grad = multiply(second_all, outer_turned, False)
     inner_grad = (act_grad * gelu_slope(inner_pre)).astype(jnp.bfloat16)
-    gathered_inner = cols_gather(inner_grad)
-    grad_innerbias = column_sums(gathered_inner)
-    mid_grad = row_reduce(gathered_inner, inner_weight, True)
-    grad_innerweight = outer_product(gathered_mid, gathered_inner)
+    mid_grad = row_reduce(multiply(inner_grad, inner_full, True)).astype(jnp.float32)
+    grad_outerweight = grad_reduce(outer_product(second_all, activated)).T
+    grad_innerbias = column_sums(inner_grad)
+    grad_innerweight = grad_reduce(outer_product(mid_all, inner_grad))
     first_up = second_grad + mid_grad
     grad_normgain = jnp.sum(first_up * first_hat, axis=0)
     grad_normbias = jnp.sum(first_up, axis=0)
     first_grad = norm_back(first_up * norm_gain, first_hat, first_scale)
     first_low = first_grad.astype(jnp.bfloat16)
     grad_mixerbias = column_sums(first_low)
-    gathered_first = rows_gather(first_low)
-    context_grad = col_reduce(gathered_first, mixer_weight).astype(jnp.bfloat16)
-    grad_mixerweight = outer_product(gathered_ctx, gathered_first)
+    first_all = rows_gather(first_low)
+    context_grad = multiply(first_all, mixer_turned, False).astype(jnp.bfloat16)
     joint_grad = attend_back(query_rows, key_rows, value_rows, log_total, context_grad, heads)
-    gathered_joint = cols_gather(joint_grad)
-    joint_bias = column_sums(gathered_joint)
-    input_part = row_reduce(gathered_joint, joint_weight, True)
-    grad_joint = outer_product(gathered_in, gathered_joint)
-    grad_inputs = first_grad + input_part
-    grad_outerweight, grad_innerweight, grad_innerbias, grad_mixerweight, grad_joint, joint_bias = (
-        lax.psum(
-            (
-                grad_outerweight,
-                grad_innerweight,
-                grad_innerbias,
-                grad_mixerweight,
-                grad_joint,
-                joint_bias,
-            ),
-            "dp",
+    input_part = multiply(joint_grad, joint_weight, True)
+    own_part = lax.dynamic_slice_in_dim(input_part, row_at * chunk, chunk, axis=0) + first_grad
+    input_part = lax.dynamic_update_slice_in_dim(input_part, own_part, row_at * chunk, axis=0)
+    grad_inputs = transposed(row_reduce(input_part, 1)).astype(jnp.float32)
+    joint_bias = column_sums(joint_grad)
+    grad_attention = grad_reduce(
+        jnp.concatenate(
+            [outer_product(input_all, joint_grad), outer_product(first_all, context)], axis=1
         )
     )
-    grad_normgain, grad_normbias, grad_finalgain, grad_finalbias, grad_mixerbias, grad_outerbias = (
-        lax.psum(
-            (
+    grad_joint = grad_attention[:, : 3 * head_width]
+    grad_mixerweight = grad_attention[:, 3 * head_width :].T
+    grad_innerbias, joint_bias = lax.psum((grad_innerbias, joint_bias), ("dp", "col"))
+    sums = lax.psum(
+        jnp.stack(
+            [
                 grad_normgain,
                 grad_normbias,
                 grad_finalgain,
                 grad_finalbias,
                 grad_mixerbias,
                 grad_outerbias,
-            ),
-            ("dp", "row"),
-        )
+            ]
+        ),
+        ("dp", "row", "col"),
+    )
+    sums = lax.dynamic_slice_in_dim(sums, col_at * width, width, axis=1)
+    grad_normgain, grad_normbias, grad_finalgain, grad_finalbias, grad_mixerbias, grad_outerbias = (
+        sums[i] for i in range(6)
     )
     grad_queryweight = grad_joint[:, :head_width]
     grad_keyweight = grad_joint[:, head_width : 2 * head_width]

time: 1860 us -> 680 us (0.37)
  waiting for transfers between devices: 1610 us -> 393 us
  blocking collectives: 58.3 us -> 99.3 us
  starting transfers between devices: 1.46 us -> 35.3 us
  matrix products: 105 us -> 76.6 us
  other arithmetic: 47.4 us -> 27.4 us
    reduce_scatter x8 -> x7, waiting for transfers between devices: 1030 us -> 143 us  [the longest x3 104 us: grad_reduce(): lax.psum_scatter(partial.astype(jnp.bfloat16), 'col', scatter_dimension=0...]
    all_gather x4 -> x3, waiting for transfers between devices: 438 us -> 103 us  [cols_gather(): return lax.all_gather(block, 'col', axis=0, tiled=True)]
    psum x1, waiting for transfers between devices: 48.9 us -> 7.24 us  [grad_reduce(): return lax.psum(scattered, 'dp').astype(jnp.float32)]
    ppermute x0 -> x4, waiting for transfers between devices: none -> 36.5 us  [transposed(): return lax.ppermute(block, ('row', 'col'), pairs)]
    all_gather x4 -> x3, waiting for transfers between devices: 92.1 us -> 58.4 us  [rows_gather(): return lax.all_gather(block, 'row', axis=0, tiled=True)]
    all_gather x0 -> x1, waiting for transfers between devices: none -> 31.2 us  [local(): input_all = lax.all_gather(transposed(inputs), 'row', axis=1, tiled=True)]
    psum x6 -> x2, blocking collectives: 58.3 us -> 74.1 us  [the longest x1 40.5 us: local(): lax.psum(jnp.stack([grad_normgain, grad_normbias, grad_finalgain, grad_fi...]
  transfers between devices with their start and end apart: 17 -> 20, of which waited for: 17 -> 15; matrix products, arithmetic and copies ran while one was open for 2% -> 10% of each run, Pallas kernels for 0% -> 0%
where the time goes in v1:
time: 680 us; the launch traced here: 670 us
  waiting for transfers between devices  393 us (58%)
  blocking collectives  99.3 us (15%)
  matrix products  76.6 us (11%)
  starting transfers between devices  35.3 us (5%)
  other arithmetic  27.4 us (4%)
  local copies, waits for them, and re-layouts  24 us (4%)
  between operations  15 us (2%)
    reduce_scatter x3, waiting for transfers between devices, grad_reduce(): lax.psum_scatter(partial.astype(jnp.bfloat16), 'col', scatter_dimension=0...  104 us
    all_gather x3, waiting for transfers between devices, cols_gather(): return lax.all_gather(block, 'col', axis=0, tiled=True)  103 us
    all_gather x3, waiting for transfers between devices, rows_gather(): return lax.all_gather(block, 'row', axis=0, tiled=True)  58.4 us
    psum x1, blocking collectives, local(): lax.psum(jnp.stack([grad_normgain, grad_normbias, grad_finalgain, grad_fi...  40.5 us
    reduce_scatter x4, waiting for transfers between devices, row_reduce(): lax.psum_scatter(partial.astype(jnp.bfloat16), 'row', scatter_dimension=d...  38.1 us
    ppermute x4, waiting for transfers between devices, transposed(): return lax.ppermute(block, ('row', 'col'), pairs)  36.5 us
    psum x1, blocking collectives, local(): lax.psum((grad_innerbias, joint_bias), ('dp', 'col'))  33.6 us
    all_gather x1, waiting for transfers between devices, local(): input_all = lax.all_gather(transposed(inputs), 'row', axis=1, tiled=True)  31.2 us
  transfers between devices with their start and end apart: 20, of which 15 were waited for; matrix products, arithmetic and copies ran while one was open for 10% of the time, Pallas kernels for 0%

profile of v1, /device:TPU:24, one launch (start us, length us, event | category | flops | bytes accessed | tf_op | source)
XLA Modules:
  0.0 670.4 jit_solution(11254530869971632471)
XLA Ops:
  8.2 1.0 copy.82
  10.3 1.7 pad_maximum_fusion.1
  12.1 2.5 collective-permute-start
  14.6 23.6 %collective-permute-done = bf16[1024,256]{1,0:T(8,128)(2,1)S(1)} collective-permute-done((bf16[1024,256]{1,0:T(8,128)(2,1)}, bf16[1024,256]{1,0:T(8,128)(2,1)S(1)}, u32[]{:S(2)}, u32[]{:S(2)}) %collective-permute-start) | collective-permute-done | bytes 524320 | tf_op jit(solution)/shard_map/ppermute | solution.py:49
  39.1 32.8 %all-gather.10.cloned.1.call-done = bf16[1024,1024]{0,1:T(8,128)(2,1)} async-done(((bf16[256,1024]{0,1:T(8,128)(2,1)}), bf16[1024,1024]{0,1:T(8,128)(2,1)}) %all-gather.10.cloned.1.call-update) | async-done | bytes 2097168 | tf_op jit(solution)/shard_map/all_gather | solution.py:41
  71.8 31.2 %all-gather.8.cloned.1.call-done = bf16[1024,1024]{1,0:T(8,128)(2,1)} async-done(((bf16[1024,256]{1,0:T(8,128)(2,1)}), bf16[1024,1024]{1,0:T(8,128)(2,1)}) %all-gather.8.cloned.1.call-update) | async-done | bytes 2097168 | tf_op jit(solution)/shard_map/all_gather | solution.py:173
  103.0 3.9 convolution_bitcast_fusion
  106.9 1.6 copy-done.10
  109.0 1.7 fusion.43
  111.5 1.3 multiply_reduce_fusion.1
  112.9 1.4 fusion
  114.3 1.8 copy-done
  116.1 1.9 fusion.40
  119.5 3.2 convolution_convert_fusion.4
  123.5 13.1 %all_gather.26 = f32[6,1024]{1,0:T(8,128)S(1)} all-gather(f32[6,256]{1,0:T(8,128)S(1)} %stack.42), channel_id=1, replica_groups=mesh['dp'=2,'row'=4,'col'=4] {'col'}, dimensions={1}, use_global_device_ids=true | all-gather | bytes 30720 | tf_op jit(solution)/shard_map/all_gather | solution.py:181
  136.6 17.7 %reduce-scatter.8.cloned.1.call-done = bf16[256,1024]{1,0:T(8,128)(2,1)} async-done(((bf16[1024,1024]{1,0:T(8,128)(2,1)}), bf16[256,1024]{1,0:T(8,128)(2,1)}) %reduce-scatter.8.cloned.1.call-update) | async-done | bytes 524304 | tf_op jit(solution)/shard_map/reduce_scatter | solution.py:53
  154.3 1.3 fusion.45
  155.6 1.4 multiply_reduce_fusion.7
  157.0 2.2 fusion.44
  160.1 39.5 %all-gather.14.cloned.1.call-done = bf16[1024,1024]{1,0:T(8,128)(2,1)} async-done(((bf16[256,1024]{1,0:T(8,128)(2,1)}), bf16[1024,1024]{1,0:T(8,128)(2,1)}) %all-gather.14.cloned.1.call-update) | async-done | bytes 2097168 | tf_op jit(solution)/shard_map/all_gather | solution.py:41
  199.6 25.6 %all-gather.12.cloned.1.call-done = bf16[1024,1024]{1,0:T(8,128)(2,1)} async-done(((bf16[256,1024]{1,0:T(8,128)(2,1)}), bf16[1024,1024]{1,0:T(8,128)(2,1)}) %all-gather.12.cloned.1.call-update) | async-done | bytes 2097168 | tf_op jit(solution)/shard_map/all_gather | solution.py:37
  225.2 14.5 %fusion.6 = (bf16[1024,1024]{1,0:T(8,128)(2,1)}, f32[1024,1024]{1,0:T(8,128)}) fusion(f32[1024]{0:T(1024)S(1)} %copy-done.30, bf16[1024,1024]{1,0:T(8,128)(2,1)} %all-gather.12.cloned.1.call-done, bf16[1024,1024]{1,0:T(8,128)(2,1)} %all-gather.14.cloned.1.call-done), kind=kOutput, calls=%fused_computation.13 | convolution fusion | flops 2216689664 | bytes 10489856 | tf_op jit(solution)/shard_map/dot_general | solution.py:21
  239.7 30.7 %all-gather.16.cloned.1.call-done = bf16[1024,1024]{0,1:T(8,128)(2,1)} async-done(((bf16[256,1024]{0,1:T(8,128)(2,1)}), bf16[1024,1024]{0,1:T(8,128)(2,1)}) %all-gather.16.cloned.1.call-update) | async-done | bytes 2097168 | tf_op jit(solution)/shard_map/all_gather | solution.py:41
  270.3 6.0 convolution_convert_fusion.3
  276.3 5.8 collective-permute-start.2
  282.1 13.0 %collective-permute-done.2 = bf16[1024,256]{1,0:T(8,128)(2,1)} collective-permute-done((bf16[1024,256]{1,0:T(8,128)(2,1)S(1)}, bf16[1024,256]{1,0:T(8,128)(2,1)}, u32[]{:S(2)}, u32[]{:S(2)}) %collective-permute-start.2) | collective-permute-done | bytes 524320 | tf_op jit(solution)/shard_map/ppermute | solution.py:49
  295.1 9.9 %all-to-all-start.1 = ((bf16[4,256,256]{2,1,0:T(8,128)(2,1)}), bf16[4,256,256]{2,1,0:T(8,128)(2,1)S(1)}, u32[]{:S(2)}, u32[]{:S(2)}) async-start(bf16[4,256,256]{2,1,0:T(8,128)(2,1)} %bitcast.18), calls=%async_computation.3 | async-start | bytes 1048576 | tf_op jit(solution)/shard_map/all_to_all | solution.py:190
  305.1 12.7 %all-to-all-done.1 = bf16[4,256,256]{2,1,0:T(8,128)(2,1)S(1)} async-done(((bf16[4,256,256]{2,1,0:T(8,128)(2,1)}), bf16[4,256,256]{2,1,0:T(8,128)(2,1)S(1)}, u32[]{:S(2)}, u32[]{:S(2)}) %all-to-all-start.1) | async-done | bytes 524320 | tf_op jit(solution)/shard_map/all_to_all | solution.py:190
  318.3 1.8 fusion.72
  320.8 1.4 fusion.71
  322.3 22.4 %all-gather.18.cloned.1.call-done = bf16[1024,1024]{1,0:T(8,128)(2,1)} async-done(((bf16[256,1024]{1,0:T(8,128)(2,1)}), bf16[1024,1024]{1,0:T(8,128)(2,1)}) %all-gather.18.cloned.1.call-update) | async-done | bytes 2097168 | tf_op jit(solution)/shard_map/all_gather | solution.py:37
  344.7 6.5 fusion.12
  351.2 1.4 copy-done.14
  352.5 3.7 convolution_convert_fusion.2
  356.3 11.2 %all-gather.20.cloned.1.call-start = ((), (), s32[]{:S(2)}) async-start(), calls=%async_computation.18 | async-start | bytes 2621440 | tf_op jit(solution)/shard_map/all_gather | solution.py:37
  367.5 20.3 %reduce-scatter.12.cloned.1.call-done = bf16[256,1024]{1,0:T(8,128)(2,1)} async-done(((bf16[1024,1024]{1,0:T(8,128)(2,1)}), bf16[256,1024]{1,0:T(8,128)(2,1)}) %reduce-scatter.12.cloned.1.call-update) | async-done | bytes 524304 | tf_op jit(solution)/shard_map/reduce_scatter | solution.py:53
  387.9 1.9 multiply_reduce_fusion.3
  389.7 2.5 fusion.70
  392.3 5.9 convolution_convert_fusion.1
  398.4 6.2 convolution_convert_fusion
  404.6 10.4 %all-gather.20.cloned.1.call-done = bf16[1024,1024]{1,0:T(8,128)(2,1)} async-done(((bf16[256,1024]{1,0:T(8,128)(2,1)}), bf16[1024,1024]{1,0:T(8,128)(2,1)}) %all-gather.20.cloned.1.call-update) | async-done | bytes 2097168 | tf_op jit(solution)/shard_map/all_gather | solution.py:37
  415.0 2.4 convolution_convert_fusion.7
  418.5 5.0 fusion.37
  424.1 5.3 multiply_reduce_fusion
  430.1 2.4 multiply_convert_fusion
  434.0 1.4 fusion.35
  437.0 1.8 fusion.23
  438.9 1.5 pad_maximum_fusion
  440.7 3.3 fusion.24
  444.2 1.7 convert_element_type.128
  445.9 12.1 %all_to_all.32 = bf16[256,4,256]{2,0,1:T(8,128)(2,1)} all-to-all(bf16[256,4,256]{2,0,1:T(8,128)(2,1)S(1)} %bitcast.132), channel_id=1, replica_groups=mesh['dp'=2,'row'=4,'col'=4] {'row'}, dimensions={1} | all-to-all | bytes 1048576 | tf_op jit(solution)/shard_map/all_to_all | solution.py:212
  458.0 1.9 collective-permute-start.1
  459.9 55.8 %reduce-scatter.20.cloned.1.call-done = bf16[256,1024]{1,0:T(8,128)(2,1)} async-done(((bf16[1024,1024]{1,0:T(8,128)(2,1)}), bf16[256,1024]{1,0:T(8,128)(2,1)}) %reduce-scatter.20.cloned.1.call-update) | async-done | bytes 524304 | tf_op jit(solution)/shard_map/reduce_scatter | solution.py:59
  515.8 48.6 %reduce-scatter.16.cloned.1.call-done = bf16[256,1024]{0,1:T(8,128)(2,1)} async-done(((bf16[1024,1024]{0,1:T(8,128)(2,1)}), bf16[256,1024]{0,1:T(8,128)(2,1)}) %reduce-scatter.16.cloned.1.call-update) | async-done | bytes 524304 | tf_op jit(solution)/shard_map/reduce_scatter | solution.py:59
  564.6 2.0 fusion.56
  566.9 40.5 %psum.44 = f32[6,1024]{1,0:T(8,128)S(1)} all-reduce(f32[6,1024]{1,0:T(8,128)S(1)} %stack.47), channel_id=1, replica_groups=mesh['dp'=2,'row'=4,'col'=4] {'dp','row','col'}, use_global_device_ids=true, to_apply=%region_22.0 | all-reduce | flops 6144 | bytes 49152 | tf_op jit(solution)/shard_map/psum | solution.py:248
  607.4 2.9 collective-permute-start.3
  611.6 33.6 %all-reduce = (f32[768]{0:T(1024)S(1)}, f32[1024]{0:T(1024)}) all-reduce(f32[768]{0:T(1024)S(1)} %convolution_reduce_fusion, f32[1024]{0:T(1024)S(1)} %bitcast.161), channel_id=1, replica_groups=mesh['dp'=2,'row'=4,'col'=4] {'dp','col'}, use_global_device_ids=true, to_apply=%region_17.0 | all-reduce | flops 1792 | bytes 14336 | tf_op jit(solution)/shard_map/psum | solution.py:247
  645.7 1.0 convert_element_type.129
  646.8 7.2 %all-reduce.4.cloned.1.call-done = (bf16[1024,256]{0,1:T(8,128)(2,1)}, bf16[256,1024]{0,1:T(8,128)(2,1)}, bf16[256,1024]{1,0:T(8,128)(2,1)}) async-done(((bf16[1024,256]{0,1:T(8,128)(2,1)}, bf16[256,1024]{0,1:T(8,128)(2,1)}, bf16[256,1024]{1,0:T(8,128)(2,1)}), (bf16[1024,256]{0,1:T(8,128)(2,1)}, bf16[256,1024]{0,1:T(8,128)(2,1)}, bf16[256,1024]{1,0:T(8,128)(2,1)})) %all-reduce.4.cloned.1.call-update) | async-done | bytes 1572880 | tf_op jit(solution)/shard_map/psum | solution.py:62
  654.0 1.1 fusion.73
  655.2 1.1 convert_element_type.130
  656.3 2.2 copy.106
  661.8 1.1 convert_element_type.132
  (149 shorter events, 20.8 us)
Async XLA Ops:
  7.2 64.7 %all-gather.10.cloned.1.call-start = ((), (), s32[]{:S(2)}) async-start(), calls=%async_computation.10 | async-start | bytes 2621440 | tf_op jit(solution)/shard_map/all_gather | solution.py:41
  12.0 91.0 %all-gather.8.cloned.1.call-start = ((), (), s32[]{:S(2)}) async-start(), calls=%async_computation.9 | async-start | bytes 2621440 | tf_op jit(solution)/shard_map/all_gather | solution.py:173
  12.1 26.1 %collective-permute-start = (bf16[1024,256]{1,0:T(8,128)(2,1)}, bf16[1024,256]{1,0:T(8,128)(2,1)S(1)}, u32[]{:S(2)}, u32[]{:S(2)}) collective-permute-start(bf16[1024,256]{1,0:T(8,128)(2,1)} %param.17), channel_id=1, source_target_pairs={{0,0},{1,4},{2,8},{3,12},{4,1},{5,5},{6,9},{7,13},{8,2},{9,6},{10,... | collective-permute-start | bytes 1572872 | tf_op jit(solution)/shard_map/ppermute | solution.py:49
  38.2 0.8 copy-start.18
  39.0 70.0 %copy-start.19 = (f32[256]{0:T(256)S(1)}, f32[256]{0:T(256)}, u32[]{:S(2)}) copy-start(f32[256]{0:T(256)} %param.22) | copy-start | bytes 3076
  39.0 70.0 %copy-start.20 = (f32[256]{0:T(256)S(1)}, f32[256]{0:T(256)}, u32[]{:S(2)}) copy-start(f32[256]{0:T(256)} %param.19) | copy-start | bytes 3076
  39.0 115.3 %reduce-scatter.8.cloned.1.call-start = ((), (), s32[]{:S(2)}) async-start(), calls=%async_computation.11 | async-start | bytes 2621440 | tf_op jit(solution)/shard_map/reduce_scatter | solution.py:53
  106.9 1.6 copy-start.10
  111.1 3.2 copy-start.11
  111.5 1.3 copy-start.2
  112.9 3.3 copy-start
  118.0 5.3 copy-start.21
  118.0 5.3 copy-start.22
  118.0 5.3 copy-start.23
  118.1 5.3 copy-start.24
  118.1 5.3 copy-start.25
  118.1 5.3 copy-start.26
  118.1 36.2 %copy-start.6 = (bf16[1024,1024]{1,0:T(8,128)(2,1)S(1)}, bf16[1024,1024]{1,0:T(8,128)(2,1)}, u32[]{:S(2)}) copy-start(bf16[1024,1024]{1,0:T(8,128)(2,1)} %all-gather.8.cloned.1.call-done) | copy-start | bytes 6291460
  118.7 0.8 copy-start.15
  122.7 102.5 %copy-start.30 = (f32[1024]{0:T(1024)S(1)}, f32[1024]{0:T(1024)}, u32[]{:S(2)}) copy-start(f32[1024]{0:T(1024)} %param.28) | copy-start | bytes 12292
  122.7 76.9 %all-gather.14.cloned.1.call-start = ((), (), s32[]{:S(2)}) async-start(), calls=%async_computation.13 | async-start | bytes 2621440 | tf_op jit(solution)/shard_map/all_gather | solution.py:41
  123.3 101.9 %all-gather.12.cloned.1.call-start = ((), (), s32[]{:S(2)}) async-start(), calls=%async_computation.12 | async-start | bytes 2621440 | tf_op jit(solution)/shard_map/all_gather | solution.py:37
  159.2 111.1 %all-gather.16.cloned.1.call-start = ((), (), s32[]{:S(2)}) async-start(), calls=%async_computation.14 | async-start | bytes 2621440 | tf_op jit(solution)/shard_map/all_gather | solution.py:41
  159.8 158.5 %reduce-scatter.10.cloned.1.call-start = ((), (), s32[]{:S(2)}) async-start(), calls=%async_computation.15 | async-start | bytes 2621440 | tf_op jit(solution)/shard_map/reduce_scatter | solution.py:53
  270.3 6.0 copy-start.29
  276.3 41.9 %copy-start.1 = (bf16[256,1024]{1,0:T(8,128)(2,1)S(1)}, bf16[256,1024]{1,0:T(8,128)(2,1)}, u32[]{:S(2)}) copy-start(bf16[256,1024]{1,0:T(8,128)(2,1)} %reduce-scatter.8.cloned.1.call-done) | copy-start | bytes 1572868
  276.3 18.8 %collective-permute-start.2 = (bf16[1024,256]{1,0:T(8,128)(2,1)S(1)}, bf16[1024,256]{1,0:T(8,128)(2,1)}, u32[]{:S(2)}, u32[]{:S(2)}) collective-permute-start(bf16[1024,256]{1,0:T(8,128)(2,1)S(1)} %copy-done.29), channel_id=1, source_target_pairs={{0,0},{1,4},{2,8},{3,12},{4,1},{5,5},{6,9},{7,13},{8,2},{9,6},{10,... | collective-permute-start | bytes 1572872 | tf_op jit(solution)/shard_map/ppermute | solution.py:49
  295.1 22.6 %all-to-all-start.1 = ((bf16[4,256,256]{2,1,0:T(8,128)(2,1)}), bf16[4,256,256]{2,1,0:T(8,128)(2,1)S(1)}, u32[]{:S(2)}, u32[]{:S(2)}) async-start(bf16[4,256,256]{2,1,0:T(8,128)(2,1)} %bitcast.18), calls=%async_computation.3 | async-start | bytes 1048576 | tf_op jit(solution)/shard_map/all_to_all | solution.py:190
  305.0 39.6 %all-gather.18.cloned.1.call-start = ((), (), s32[]{:S(2)}) async-start(), calls=%async_computation.16 | async-start | bytes 2621440 | tf_op jit(solution)/shard_map/all_gather | solution.py:37
  322.2 65.6 %reduce-scatter.12.cloned.1.call-start = ((), (), s32[]{:S(2)}) async-start(), calls=%async_computation.17 | async-start | bytes 2621440 | tf_op jit(solution)/shard_map/reduce_scatter | solution.py:53
  344.7 7.9 %copy-start.27 = (bf16[1024,1024]{1,0:T(8,128)(2,1)S(1)}, bf16[1024,1024]{1,0:T(8,128)(2,1)}, u32[]{:S(2)}) copy-start(bf16[1024,1024]{1,0:T(8,128)(2,1)} %all-gather.14.cloned.1.call-done) | copy-start | bytes 6291460
  351.1 1.4 copy-start.14
  356.3 58.7 %all-gather.20.cloned.1.call-start = ((), (), s32[]{:S(2)}) async-start(), calls=%async_computation.18 | async-start | bytes 2621440 | tf_op jit(solution)/shard_map/all_gather | solution.py:37
  392.3 67.7 %reduce-scatter.18.cloned.1.call-start = ((), (), s32[]{:S(2)}) async-start(), calls=%async_computation.21 | async-start | bytes 2621440 | tf_op jit(solution)/shard_map/reduce_scatter | solution.py:59
  398.3 117.5 %reduce-scatter.20.cloned.1.call-start = ((), (), s32[]{:S(2)}) async-start(), calls=%async_computation.22 | async-start | bytes 2621440 | tf_op jit(solution)/shard_map/reduce_scatter | solution.py:59
  404.6 159.9 %reduce-scatter.16.cloned.1.call-start = ((), (), s32[]{:S(2)}) async-start(), calls=%async_computation.20 | async-start | bytes 2621440 | tf_op jit(solution)/shard_map/reduce_scatter | solution.py:59
  418.5 5.6 copy-start.12
  424.0 5.4 slice-start
  424.1 5.9 slice-start.1
  432.5 1.4 copy-start.3
  433.9 2.2 copy-start.16
  434.0 2.2 copy-start.28
  435.4 1.7 copy-start.7
  436.1 4.5 copy-start.8
  440.4 167.0 %reduce-scatter.14.cloned.1.call-start = ((), (), s32[]{:S(2)}) async-start(), calls=%async_computation.19 | async-start | bytes 2621440 | tf_op jit(solution)/shard_map/reduce_scatter | solution.py:53
  444.1 1.8 copy-start.13
  445.8 118.6 %copy-start.4 = (bf16[256,1024]{1,0:T(8,128)(2,1)S(1)}, bf16[256,1024]{1,0:T(8,128)(2,1)}, u32[]{:S(2)}) copy-start(bf16[256,1024]{1,0:T(8,128)(2,1)} %get-tuple-element.83) | copy-start | bytes 1572868
  445.8 120.8 %copy-start.5 = (bf16[256,1024]{1,0:T(8,128)(2,1)S(1)}, bf16[256,1024]{1,0:T(8,128)(2,1)}, u32[]{:S(2)}) copy-start(bf16[256,1024]{1,0:T(8,128)(2,1)} %get-tuple-element.81) | copy-start | bytes 1572868
  445.8 165.2 %copy-start.9 = (bf16[1024,768]{0,1:T(8,128)(2,1)S(1)}, bf16[1024,768]{0,1:T(8,128)(2,1)}, u32[]{:S(2)}) copy-start(bf16[1024,768]{0,1:T(8,128)(2,1)} %copy-done.8) | copy-start | bytes 4718596
  445.8 208.2 %all-reduce.4.cloned.1.call-start = ((), (), s32[]{:S(2)}) async-start(), calls=%async_computation.23 | async-start | bytes 3145728 | tf_op jit(solution)/shard_map/psum | solution.py:62
  458.0 106.6 %collective-permute-start.1 = (bf16[1024,256]{1,0:T(8,128)(2,1)}, bf16[1024,256]{1,0:T(8,128)(2,1)S(1)}, u32[]{:S(2)}, u32[]{:S(2)}) collective-permute-start(bf16[1024,256]{1,0:T(8,128)(2,1)} %bitcast.17), channel_id=1, source_target_pairs={{0,0},{1,4},{2,8},{3,12},{4,1},{5,5},{6,9},{7,13},{8,2},{9,6},{10,... | collective-permute-start | bytes 1572872 | tf_op jit(solution)/shard_map/ppermute | solution.py:49
  607.4 38.3 %collective-permute-start.3 = (bf16[1024,256]{1,0:T(8,128)(2,1)}, bf16[1024,256]{1,0:T(8,128)(2,1)S(1)}, u32[]{:S(2)}, u32[]{:S(2)}) collective-permute-start(bf16[1024,256]{1,0:T(8,128)(2,1)} %reduce-scatter.14.cloned.1.call-done), channel_id=1, source_target_pairs={{0,0},{1,4},{2,8},{3,12},{4,1},{5,5},{6,9},{7,13},{8,2},{9,6},{10,... | collective-permute-start | bytes 1572872 | tf_op jit(solution)/shard_map/ppermute | solution.py:49
  654.0 7.7 %copy-start.17 = (bf16[256,1024]{1,0:T(8,128)(2,1)S(1)}, bf16[256,1024]{1,0:T(8,128)(2,1)}, u32[]{:S(2)}) copy-start(bf16[256,1024]{1,0:T(8,128)(2,1)} %get-tuple-element.80) | copy-start | bytes 1572868
Sparse Core Ops, SparseCore 0:
  12.1 59.6 all-gather.9
  74.0 29.0 all-gather.7
  122.9 31.4 reduce-scatter.7
  155.8 43.7 all-gather.13
  201.7 23.4 all-gather.11
  226.7 43.5 all-gather.15
  276.5 40.4 reduce-scatter.9
  322.3 22.2 all-gather.17
  356.4 31.4 reduce-scatter.11
  392.4 22.5 all-gather.19
  417.4 42.0 reduce-scatter.17
  461.6 54.1 reduce-scatter.19
  518.2 46.1 reduce-scatter.15
  566.8 32.6 reduce-scatter.13
  601.9 52.0 all-reduce.3

commit v2 on v1

--- a/solution.py
+++ b/solution.py
@@ -33,33 +33,95 @@
     )[0]
 
 
-def rows_gather(block):
-    return lax.all_gather(block, "row", axis=0, tiled=True)
+def flipped_axis(block, axis, mask):
+    return lax.ppermute(block, axis, [(i, i ^ mask) for i in range(lax.axis_size(axis))])
 
 
 def cols_gather(block):
     return lax.all_gather(block, "col", axis=0, tiled=True)
 
 
-def transposed(block):
-    row_count, col_count = lax.axis_size("row"), lax.axis_size("col")
-    pairs = [
-        (r * col_count + c, c * col_count + r) for r in range(row_count) for c in range(col_count)
-    ]
-    return lax.ppermute(block, ("row", "col"), pairs)
-
-
-def row_reduce(partial, dimension=0):
-    return lax.psum_scatter(
-        partial.astype(jnp.bfloat16), "row", scatter_dimension=dimension, tiled=True
-    )
+def rows_gather(block):
+    chunks = {0: block}
+    mask = lax.axis_size("row") // 2
+    while mask:
+        held = sorted(chunks)
+        arrived = flipped_axis(jnp.concatenate([chunks[m] for m in held]), "row", mask)
+        for m, part in zip(held, jnp.split(arrived, len(held))):
+            chunks[m ^ mask] = part
+        mask //= 2
+    return jnp.concatenate([chunks[m] for m in sorted(chunks)])
+
+
+def row_reduce(partial):
+    count = lax.axis_size("row")
+    chunks = dict(enumerate(jnp.split(partial, count)))
+    mask = 1
+    while mask < count:
+        away = [m for m in sorted(chunks) if m & mask]
+        arrived = flipped_axis(
+            jnp.concatenate([chunks[m] for m in away]).astype(jnp.bfloat16), "row", mask
+        )
+        for m, part in zip(away, jnp.split(arrived, len(away))):
+            chunks[m ^ mask] = chunks[m ^ mask] + part.astype(jnp.float32)
+            del chunks[m]
+        mask *= 2
+    return chunks[0]
+
+
+def in_order(parts, at, axis):
+    stacked = jnp.stack(parts)
+    return jnp.concatenate(
+        [
+            lax.dynamic_index_in_dim(stacked, at ^ i, axis=0, keepdims=False)
+            for i in range(len(parts))
+        ],
+        axis=axis,
+    )
+
+
+def to_whole_rows(block):
+    count = lax.axis_size("row")
+    row_at, col_at = lax.axis_index("row"), lax.axis_index("col")
+    chunks = jnp.stack(jnp.split(block, count))
+    parts = []
+    for k in range(count):
+        sent = lax.dynamic_index_in_dim(chunks, col_at ^ k, axis=0, keepdims=False)
+        pairs = [(r * count + c, (c ^ k) * count + r) for r in range(count) for c in range(count)]
+        parts.append(lax.ppermute(sent, ("row", "col"), pairs))
+    return in_order(parts, row_at, 1)
+
+
+def to_feature_blocks(rows):
+    count = lax.axis_size("row")
+    row_at, col_at = lax.axis_index("row"), lax.axis_index("col")
+    blocks = jnp.stack(jnp.split(rows, count, axis=1))
+    parts = []
+    for k in range(count):
+        sent = lax.dynamic_index_in_dim(blocks, row_at ^ k, axis=0, keepdims=False)
+        pairs = [(r * count + c, c * count + (r ^ k)) for r in range(count) for c in range(count)]
+        parts.append(lax.ppermute(sent, ("row", "col"), pairs))
+    return in_order(parts, col_at, 0)
+
+
+def butterfly_sum(values, axis):
+    mask = 1
+    while mask < lax.axis_size(axis):
+        values = values + flipped_axis(values, axis, mask)
+        mask *= 2
+    return values
+
+
+def replica_sum(values):
+    if lax.axis_size("dp") == 2:
+        return values.astype(jnp.float32) + flipped_axis(values, "dp", 1).astype(jnp.float32)
+    return lax.psum(values, "dp").astype(jnp.float32)
 
 
 def grad_reduce(partial):
-    scattered = lax.psum_scatter(
-        partial.astype(jnp.bfloat16), "col", scatter_dimension=0, tiled=True
-    )
-    return lax.psum(scattered, "dp").astype(jnp.float32)
+    return replica_sum(
+        lax.psum_scatter(partial.astype(jnp.bfloat16), "col", scatter_dimension=0, tiled=True)
+    )
 
 
 def normalize(total):
@@ -166,51 +228,44 @@
 ):
     head_width = query_weight.shape[1]
     heads = head_width // DH
-    row_at, col_at = lax.axis_index("row"), lax.axis_index("col")
-    chunk = inputs.shape[0] // lax.axis_size("row")
+    col_at = lax.axis_index("col")
     width = inputs.shape[1]
 
-    input_all = lax.all_gather(transposed(inputs), "row", axis=1, tiled=True)
-    attention_weights = cols_gather(
-        jnp.concatenate([query_weight, key_weight, value_weight, mixer_weight.T], axis=1)
-    )
-    joint_weight = attention_weights[:, : 3 * head_width]
-    mixer_turned = attention_weights[:, 3 * head_width :]
-    inner_full = cols_gather(inner_weight)
+    input_own = to_whole_rows(inputs)
+    input_all = rows_gather(input_own)
+    joint_weight = cols_gather(jnp.concatenate([query_weight, key_weight, value_weight], axis=1))
+    inner_group = cols_gather(jnp.concatenate([mixer_weight.T, inner_weight], axis=1))
+    mixer_turned = inner_group[:, :head_width]
+    inner_full = inner_group[:, head_width:]
     outer_turned = cols_gather(outer_weight.T)
-    vectors = lax.all_gather(
-        jnp.stack([mixer_bias, norm_gain, norm_bias, outer_bias, final_gain, final_bias]),
-        "col",
-        axis=1,
-        tiled=True,
+    vectors = jnp.stack([mixer_bias, norm_gain, norm_bias, outer_bias, final_gain, final_bias])
+    vectors = in_order(
+        [vectors] + [flipped_axis(vectors, "col", k) for k in range(1, lax.axis_size("col"))],
+        col_at,
+        1,
     )
     mixer_bias, norm_gain, norm_bias, outer_bias, final_gain, final_bias = (
         vectors[i] for i in range(6)
     )
-    upstream = lax.all_to_all(
-        transposed(cotangent), "row", split_axis=0, concat_axis=1, tiled=True
-    ).astype(jnp.float32)
-
-    input_own = lax.dynamic_slice_in_dim(input_all, row_at * chunk, chunk, axis=0)
+    upstream = to_whole_rows(cotangent).astype(jnp.float32)
+
     projected = multiply(input_all, joint_weight, False)
     query_rows = (projected[:, :head_width] + query_bias).astype(jnp.bfloat16)
     key_rows = projected[:, head_width : 2 * head_width].astype(jnp.bfloat16)
     value_rows = (projected[:, 2 * head_width :] + value_bias).astype(jnp.bfloat16)
     context, log_total = attend(query_rows, key_rows, value_rows, heads)
-    mixed = row_reduce(multiply(context, mixer_turned, True)).astype(jnp.float32)
+    mixed = row_reduce(multiply(context, mixer_turned, True))
     first_sum = input_own.astype(jnp.float32) + mixed + mixer_bias
     first_hat, first_scale = normalize(first_sum)
     first_out = first_hat * norm_gain + norm_bias
     mid_all = rows_gather(first_out.astype(jnp.bfloat16))
     inner_pre = multiply(mid_all, inner_full, False) + inner_bias
     activated = jax.nn.gelu(inner_pre, approximate=False).astype(jnp.bfloat16)
-    outer = row_reduce(multiply(activated, outer_turned, True)).astype(jnp.float32)
+    outer = row_reduce(multiply(activated, outer_turned, True))
     second_sum = first_out + outer + outer_bias
     second_hat, second_scale = normalize(second_sum)
     layer_rows = (second_hat * final_gain + final_bias).astype(jnp.bfloat16)
-    layer_out = transposed(
-        lax.all_to_all(layer_rows, "row", split_axis=1, concat_axis=0, tiled=True)
-    )
+    layer_out = to_feature_blocks(layer_rows)
     grad_finalgain = jnp.sum(upstream * second_hat, axis=0)
     grad_finalbias = jnp.sum(upstream, axis=0)
     second_grad = norm_back(upstream * final_gain, second_hat, second_scale)
@@ -219,7 +274,7 @@
     second_all = rows_gather(second_low)
     act_grad = multiply(second_all, outer_turned, False)
     inner_grad = (act_grad * gelu_slope(inner_pre)).astype(jnp.bfloat16)
-    mid_grad = row_reduce(multiply(inner_grad, inner_full, True)).astype(jnp.float32)
+    mid_grad = row_reduce(multiply(inner_grad, inner_full, True))
     grad_outerweight = grad_reduce(outer_product(second_all, activated)).T
     grad_innerbias = column_sums(inner_grad)
     grad_innerweight = grad_reduce(outer_product(mid_all, inner_grad))
@@ -232,10 +287,8 @@
     first_all = rows_gather(first_low)
     context_grad = multiply(first_all, mixer_turned, False).astype(jnp.bfloat16)
     joint_grad = attend_back(query_rows, key_rows, value_rows, log_total, context_grad, heads)
-    input_part = multiply(joint_grad, joint_weight, True)
-    own_part = lax.dynamic_slice_in_dim(input_part, row_at * chunk, chunk, axis=0) + first_grad
-    input_part = lax.dynamic_update_slice_in_dim(input_part, own_part, row_at * chunk, axis=0)
-    grad_inputs = transposed(row_reduce(input_part, 1)).astype(jnp.float32)
+    input_grad = first_grad + row_reduce(multiply(joint_grad, joint_weight, True))
+    grad_inputs = to_feature_blocks(input_grad.astype(jnp.bfloat16)).astype(jnp.float32)
     joint_bias = column_sums(joint_grad)
     grad_attention = grad_reduce(
         jnp.concatenate(
@@ -244,21 +297,24 @@
     )
     grad_joint = grad_attention[:, : 3 * head_width]
     grad_mixerweight = grad_attention[:, 3 * head_width :].T
-    grad_innerbias, joint_bias = lax.psum((grad_innerbias, joint_bias), ("dp", "col"))
-    sums = lax.psum(
-        jnp.stack(
-            [
-                grad_normgain,
-                grad_normbias,
-                grad_finalgain,
-                grad_finalbias,
-                grad_mixerbias,
-                grad_outerbias,
-            ]
-        ),
-        ("dp", "row", "col"),
-    )
-    sums = lax.dynamic_slice_in_dim(sums, col_at * width, width, axis=1)
+    row_sums = [
+        grad_normgain,
+        grad_normbias,
+        grad_finalgain,
+        grad_finalbias,
+        grad_mixerbias,
+        grad_outerbias,
+    ]
+    sums = replica_sum(
+        butterfly_sum(jnp.concatenate(row_sums + [grad_innerbias, joint_bias]), "col")
+    )
+    split_at = 6 * D
+    grad_innerbias = sums[split_at : split_at + grad_innerbias.shape[0]]
+    joint_bias = sums[split_at + grad_innerbias.shape[0] :]
+    sums = lax.dynamic_slice_in_dim(
+        sums[:split_at].reshape(6, D), col_at * width, width, axis=1
+    )
+    sums = butterfly_sum(sums, "row")
     grad_normgain, grad_normbias, grad_finalgain, grad_finalbias, grad_mixerbias, grad_outerbias = (
         sums[i] for i in range(6)
     )

time: 680 us -> 480 us (0.71)
  waiting for transfers between devices: 393 us -> 243 us
  blocking collectives: 99.3 us -> 0 us
  starting transfers between devices: 35.3 us -> 73.2 us
  local copies, waits for them, and re-layouts: 24 us -> 31.2 us
    ppermute x4 -> x43, waiting for transfers between devices: 36.5 us -> 180 us  [the longest x27 109 us: flipped_axis(): lax.ppermute(block, axis, [(i, i ^ mask) for i in range(lax.axis_size(axi...]
    reduce_scatter x3, waiting for transfers between devices: 104 us -> 0.02 us  [grad_reduce(): lax.psum_scatter(partial.astype(jnp.bfloat16), 'col', scatter_dimension=0...]
    all_gather x4 -> x0, waiting for transfers between devices: 89.6 us -> none  [the longest x3 58.4 us: rows_gather(): return lax.all_gather(block, 'row', axis=0, tiled=True)]
    psum x2 -> x0, blocking collectives: 74.1 us -> none  [the longest x1 40.5 us: local(): lax.psum(jnp.stack([grad_normgain, grad_normbias, grad_finalgain, grad_fi...]
    ppermute x4 -> x43, starting transfers between devices: 13.1 us -> 72.3 us  [the longest x27 48.9 us: flipped_axis(): lax.ppermute(block, axis, [(i, i ^ mask) for i in range(lax.axis_size(axi...]
    all_gather x3, waiting for transfers between devices: 103 us -> 62.9 us  [cols_gather(): return lax.all_gather(block, 'col', axis=0, tiled=True)]
    reduce_scatter x4 -> x0, waiting for transfers between devices: 38.1 us -> none  [row_reduce(): lax.psum_scatter(partial.astype(jnp.bfloat16), 'row', scatter_dimension=d...]
    all_gather x1 -> x0, blocking collectives: 13.1 us -> none  [local(): lax.all_gather(jnp.stack([mixer_bias, norm_gain, norm_bias, outer_bias, f...]
  transfers between devices with their start and end apart: 20 -> 49, of which waited for: 15 -> 29; matrix products, arithmetic and copies ran while one was open for 10% -> 22% of each run, Pallas kernels for 0% -> 0%
where the time goes in v2:
time: 480 us; the launch traced here: 471 us
  waiting for transfers between devices  243 us (51%)
  matrix products  74.1 us (15%)
  starting transfers between devices  73.2 us (15%)
  other arithmetic  33.4 us (7%)
  local copies, waits for them, and re-layouts  31.2 us (6%)
  between operations  16.4 us (3%)
    ppermute x27, waiting for transfers between devices, flipped_axis(): lax.ppermute(block, axis, [(i, i ^ mask) for i in range(lax.axis_size(axi...  109 us
    all_gather x3, waiting for transfers between devices, cols_gather(): return lax.all_gather(block, 'col', axis=0, tiled=True)  62.9 us
    ppermute x8, waiting for transfers between devices, to_whole_rows(): parts.append(lax.ppermute(sent, ('row', 'col'), pairs))  55 us
    ppermute x27, starting transfers between devices, flipped_axis(): lax.ppermute(block, axis, [(i, i ^ mask) for i in range(lax.axis_size(axi...  48.9 us
    dot_general x4, matrix products, multiply(): return jnp.dot(left, right, preferred_element_type=jnp.float32)  28.8 us
    ppermute x8, waiting for transfers between devices, to_feature_blocks(): parts.append(lax.ppermute(sent, ('row', 'col'), pairs))  16 us
    unnamed x212, local copies, waits for them, and re-layouts  15 us
    ppermute x8, starting transfers between devices, to_whole_rows(): parts.append(lax.ppermute(sent, ('row', 'col'), pairs))  14.2 us
  transfers between devices with their start and end apart: 49, of which 29 were waited for; matrix products, arithmetic and copies ran while one was open for 22% of the time, Pallas kernels for 0%

profile of v2, /device:TPU:24, one launch (start us, length us, event | category | flops | bytes accessed | tf_op | source)
XLA Modules:
  0.0 471.1 jit_solution(16741372677038091755)
XLA Ops:
  7.2 1.8 pad_maximum_fusion.25
  10.5 5.8 %collective-permute-start = (bf16[256,256]{1,0:T(8,128)(2,1)S(1)}, bf16[256,256]{1,0:T(8,128)(2,1)S(1)}, u32[]{:S(2)}, u32[]{:S(2)}) collective-permute-start(bf16[256,256]{1,0:T(8,128)(2,1)S(1)} %get-tuple-element.130), channel_id=1, source_target_pairs={{0,0},{1,4},{2,8},{3,12},{4,1},{5,5},{6,9},{7,13},{8,2},{9,6},{10,... | collective-permute-start | bytes 393224 | tf_op jit(solution)/shard_map/ppermute | solution.py:91
  16.5 4.8 %collective-permute-done = bf16[256,256]{1,0:T(8,128)(2,1)S(1)} collective-permute-done((bf16[256,256]{1,0:T(8,128)(2,1)S(1)}, bf16[256,256]{1,0:T(8,128)(2,1)S(1)}, u32[]{:S(2)}, u32[]{:S(2)}) %collective-permute-start) | collective-permute-done | bytes 131104 | tf_op jit(solution)/shard_map/ppermute | solution.py:91
  21.3 34.6 %collective-permute-done.1 = bf16[256,256]{1,0:T(8,128)(2,1)S(1)} collective-permute-done((bf16[256,256]{1,0:T(8,128)(2,1)S(1)}, bf16[256,256]{1,0:T(8,128)(2,1)S(1)}, u32[]{:S(2)}, u32[]{:S(2)}) %collective-permute-start.1) | collective-permute-done | bytes 131104 | tf_op jit(solution)/shard_map/ppermute | solution.py:91
  56.3 11.4 %collective-permute-done.4 = bf16[256,1024]{1,0:T(8,128)(2,1)S(1)} collective-permute-done((bf16[256,1024]{1,0:T(8,128)(2,1)S(1)}, bf16[256,1024]{1,0:T(8,128)(2,1)S(1)}, u32[]{:S(2)}, u32[]{:S(2)}) %collective-permute-start.4) | collective-permute-done | bytes 524320 | tf_op jit(solution)/shard_map/ppermute | solution.py:37
  68.4 3.2 collective-permute-start.5
  71.8 1.9 pad_maximum_fusion.13
  74.1 3.7 fusion.91
  84.1 1.9 copy-done
  86.0 2.0 fusion.41
  88.7 39.1 %all-gather.6.cloned.1.call-done = bf16[1024,1280]{1,0:T(8,128)(2,1)} async-done(((bf16[256,1280]{1,0:T(8,128)(2,1)}), bf16[1024,1280]{1,0:T(8,128)(2,1)}) %all-gather.6.cloned.1.call-update) | async-done | bytes 2621456 | tf_op jit(solution)/shard_map/all_gather | solution.py:41
  127.8 1.8 fusion.108
  130.0 2.6 collective-permute-done.6
  141.7 2.6 collective-permute-done.10
  145.5 2.3 collective-permute-done.7
  147.9 1.7 fusion.96
  150.8 1.8 collective-permute-start.11
  152.5 11.4 %collective-permute-done.11 = bf16[256,1024]{1,0:T(8,128)(2,1)S(1)} collective-permute-done((bf16[256,1024]{1,0:T(8,128)(2,1)S(1)}, bf16[256,1024]{1,0:T(8,128)(2,1)S(1)}, u32[]{:S(2)}, u32[]{:S(2)}) %collective-permute-start.11) | collective-permute-done | bytes 524320 | tf_op jit(solution)/shard_map/ppermute | solution.py:37
  165.7 2.5 collective-permute-done.12
  170.4 16.2 %fusion.6 = (bf16[1024,1024]{1,0:T(8,128)(2,1)}, f32[1024,1024]{1,0:T(8,128)}) fusion(f32[1024]{0:T(1024)S(1)} %copy-done.92, bf16[1024,1280]{1,0:T(8,128)(2,1)} %all-gather.6.cloned.1.call-done, bf16[256,1024]{1,0:T(8,128)(2,1)S(1)} %get-tuple-element.85, bf16[256,1024]{1,0:T(8,128)(2,1)S(1)} %collective-permute-done.11, ...), kind=kOutput, calls=%fused_computation.13 | convolution fusion | flops 2225078272 | bytes 10489856 | tf_op jit(solution)/shard_map/dot_general | solution.py:21
  186.6 23.8 %all-gather.8.cloned.1.call-done = bf16[1024,1024]{0,1:T(8,128)(2,1)} async-done(((bf16[256,1024]{0,1:T(8,128)(2,1)}), bf16[1024,1024]{0,1:T(8,128)(2,1)}) %all-gather.8.cloned.1.call-update) | async-done | bytes 2097168 | tf_op jit(solution)/shard_map/all_gather | solution.py:41
  210.4 4.5 fusion.109
  216.0 1.8 collective-permute-done.13
  219.5 4.6 collective-permute-start.19
  224.2 2.2 collective-permute-start.20
  229.4 12.5 %collective-permute-done.20 = bf16[256,256]{1,0:T(8,128)(2,1)S(1)} collective-permute-done((bf16[256,256]{1,0:T(8,128)(2,1)S(1)}, bf16[256,256]{1,0:T(8,128)(2,1)S(1)}, u32[]{:S(2)}, u32[]{:S(2)}) %collective-permute-start.20) | collective-permute-done | bytes 131104 | tf_op jit(solution)/shard_map/ppermute | solution.py:91
  246.4 4.8 %collective-permute-start.23 = (bf16[256,1024]{1,0:T(8,128)(2,1)S(1)}, bf16[256,1024]{1,0:T(8,128)(2,1)S(1)}, u32[]{:S(2)}, u32[]{:S(2)}) collective-permute-start(bf16[256,1024]{1,0:T(8,128)(2,1)S(1)} %get-tuple-element.89), channel_id=1, source_target_pairs={{0,8},{4,12},{8,0},{12,4},{1,9},{5,13},{9,1},{13,5},{2,10},{6,14},... | collective-permute-start | bytes 1572872 | tf_op jit(solution)/shard_map/ppermute | solution.py:37
  251.2 9.1 %collective-permute-done.23 = bf16[256,1024]{1,0:T(8,128)(2,1)S(1)} collective-permute-done((bf16[256,1024]{1,0:T(8,128)(2,1)S(1)}, bf16[256,1024]{1,0:T(8,128)(2,1)S(1)}, u32[]{:S(2)}, u32[]{:S(2)}) %collective-permute-start.23) | collective-permute-done | bytes 524320 | tf_op jit(solution)/shard_map/ppermute | solution.py:37
  260.4 2.6 collective-permute-done.24
  264.1 3.7 convolution_convert_fusion
  268.0 7.2 %fusion.12 = bf16[1024,1024]{1,0:T(8,128)(2,1)S(1)} fusion(f32[1024,1024]{1,0:T(8,128)} %get-tuple-element.161, bf16[1024,1024]{0,1:T(8,128)(2,1)} %all-gather.8.cloned.1.call-done, f32[1024]{0:T(1024)S(1)} %copy-done.93, bf16[256,1024]{1,0:T(8,128)(2,1)} %copy-done.48, bf16[256,1024]{1,0:T(8,128)(2,1)} %copy-done.46, bf16[256,1024]{1,0:T(8,128)(2,1)} %copy-done.47, ...), kind=kOutput, calls=%fused_computation.19 | convolution fusion | flops 2167406592 | bytes 10489856 | tf_op jit(solution)/shard_map/dot_general | solution.py:21
  275.1 2.4 fusion.110
  278.0 2.5 collective-permute-done.25
  280.7 1.8 collective-permute-start.26
  283.3 11.4 %collective-permute-done.26 = bf16[256,1024]{1,0:T(8,128)(2,1)S(1)} collective-permute-done((bf16[256,1024]{1,0:T(8,128)(2,1)S(1)}, bf16[256,1024]{1,0:T(8,128)(2,1)S(1)}, u32[]{:S(2)}, u32[]{:S(2)}) %collective-permute-start.26) | collective-permute-done | bytes 524320 | tf_op jit(solution)/shard_map/ppermute | solution.py:37
  294.9 2.6 multiply_reduce_fusion.2
  298.8 1.7 collective-permute-start.27
  300.6 3.8 convolution_convert_fusion.1
  304.4 7.7 %collective-permute-done.27 = bf16[256,1024]{1,0:T(8,128)(2,1)S(1)} collective-permute-done((bf16[256,1024]{1,0:T(8,128)(2,1)S(1)}, bf16[256,1024]{1,0:T(8,128)(2,1)S(1)}, u32[]{:S(2)}, u32[]{:S(2)}) %collective-permute-start.27) | collective-permute-done | bytes 524320 | tf_op jit(solution)/shard_map/ppermute | solution.py:37
  313.1 2.6 fusion.72
  319.6 1.7 convolution_convert_fusion.4
  324.4 5.0 %fusion.38 = bf16[2,512,4,64]{1,3,2,0:T(8,128)(2,1)S(1)} fusion(bf16[2,512,4,64]{1,3,2,0:T(8,128)(2,1)S(1)} %copy.61, f32[2,4,512,512]{2,3,1,0:T(8,128)} %copy-done, f32[2,4,512]{2,1,0:T(4,128)S(1)} %bitcast.221), kind=kOutput, calls=%fused_computation.66 | convolution fusion | flops 274989056 | bytes 9453568 | tf_op jit(solution)/shard_map/bhqk,bqhd->bkhd/dot_general | solution.py:186
  330.1 4.8 %multiply_reduce_fusion = (f32[2,4,512]{2,1,0:T(4,128)S(1)}, f32[2,4,512,512]{2,3,1,0:T(8,128)S(1)}) fusion(f32[2,4,512,512]{2,3,1,0:T(8,128)} %copy-done, f32[2,4,512]{2,1,0:T(4,128)S(1)} %bitcast.222, bf16[2,512,4,64]{1,3,2,0:T(8,128)(2,1)S(1)} %copy.61, bf16[2,512,4,64]{1,3,2,0:T(8,128)(2,1)S(1)} %copy-done.10), kind=kOutput, calls=%fused_computation.1 | convolution fusion | flops 276819968 | bytes 17858560 | tf_op jit(solution)/shard_map/bqhd,bkhd->bhqk/dot_general | solution.py:189
  336.0 2.4 multiply_convert_fusion
  344.3 5.2 %convolution_convert_fusion.2 = bf16[1024,768]{0,1:T(8,128)(2,1)S(1)} fusion(bf16[1024,768]{0,1:T(8,128)(2,1)S(1)} %constant_dynamic-update-slice_fusion, bf16[256,1024]{1,0:T(8,128)(2,1)S(1)} %copy-done.32, bf16[256,1024]{1,0:T(8,128)(2,1)S(1)} %copy-done.28, bf16[256,1024]{1,0:T(8,128)(2,1)S(1)} %copy-done.30, bf16[256,256]{1,0:T(8,128)(2,1)S(1)} %copy-done.19, ...), kind=kOutput, calls=%fused_computation.49 | convolution fusion | flops 1626079232 | bytes 5242880 | tf_op jit(solution)/shard_map/dot_general | solution.py:25
  351.6 3.9 fusion.111
  357.8 3.3 collective-permute-start.36
  361.2 2.0 collective-permute-done.36
  363.2 2.5 collective-permute-start.37
  365.8 2.2 collective-permute-start.15
  367.9 2.5 collective-permute-start.16
  371.2 7.5 %collective-permute-done.15 = bf16[256,256]{1,0:T(8,128)(2,1)S(1)} collective-permute-done((bf16[256,256]{1,0:T(8,128)(2,1)S(1)}, bf16[256,256]{1,0:T(8,128)(2,1)S(1)}, u32[]{:S(2)}, u32[]{:S(2)}) %collective-permute-start.15) | collective-permute-done | bytes 131104 | tf_op jit(solution)/shard_map/ppermute | solution.py:103
  379.5 5.9 %collective-permute-done.16 = bf16[256,256]{1,0:T(8,128)(2,1)S(1)} collective-permute-done((bf16[256,256]{1,0:T(8,128)(2,1)S(1)}, bf16[256,256]{1,0:T(8,128)(2,1)S(1)}, u32[]{:S(2)}, u32[]{:S(2)}) %collective-permute-start.16) | collective-permute-done | bytes 131104 | tf_op jit(solution)/shard_map/ppermute | solution.py:103
  385.4 2.6 collective-permute-done.18
  388.2 15.9 %collective-permute-start.39 = (f32[6,256]{1,0:T(8,128)S(1)}, f32[6,256]{1,0:T(8,128)S(1)}, u32[]{:S(2)}, u32[]{:S(2)}) collective-permute-start(f32[6,256]{1,0:T(8,128)S(1)} %constant_dynamic-slice_fusion), channel_id=1, source_target_pairs={{0,4},{4,0},{8,12},{12,8},{1,5},{5,1},{9,13},{13,9},{2,6},{6,2},{1... | collective-permute-start | bytes 18440 | tf_op jit(solution)/shard_map/ppermute | solution.py:37
  404.1 2.2 fusion.46
  406.3 2.0 collective-permute-start.40
  409.5 11.0 %collective-permute-done.40 = f32[6,256]{1,0:T(8,128)S(1)} collective-permute-done((f32[6,256]{1,0:T(8,128)S(1)}, f32[6,256]{1,0:T(8,128)S(1)}, u32[]{:S(2)}, u32[]{:S(2)}) %collective-permute-start.40) | collective-permute-done | bytes 6176 | tf_op jit(solution)/shard_map/ppermute | solution.py:37
  421.2 2.0 collective-permute-start.41
  424.9 1.9 collective-permute-start.31
  426.9 1.8 collective-permute-start.32
  428.7 7.6 %collective-permute-done.42 = bf16[256,1024]{1,0:T(8,128)(2,1)} collective-permute-done((bf16[256,1024]{1,0:T(8,128)(2,1)}, bf16[256,1024]{1,0:T(8,128)(2,1)}, u32[]{:S(2)}, u32[]{:S(2)}) %collective-permute-start.42) | collective-permute-done | bytes 524320 | tf_op jit(solution)/shard_map/ppermute | solution.py:37
  437.5 8.1 %collective-permute-done.41 = bf16[256,1024]{1,0:T(8,128)(2,1)S(1)} collective-permute-done((bf16[256,1024]{1,0:T(8,128)(2,1)}, bf16[256,1024]{1,0:T(8,128)(2,1)S(1)}, u32[]{:S(2)}, u32[]{:S(2)}) %collective-permute-start.41) | collective-permute-done | bytes 524320 | tf_op jit(solution)/shard_map/ppermute | solution.py:37
  450.4 9.9 %collective-permute-done.35 = bf16[256,1024]{0,1:T(8,128)(2,1)S(1)} collective-permute-done((bf16[256,1024]{0,1:T(8,128)(2,1)}, bf16[256,1024]{0,1:T(8,128)(2,1)S(1)}, u32[]{:S(2)}, u32[]{:S(2)}) %collective-permute-start.35) | collective-permute-done | bytes 524320 | tf_op jit(solution)/shard_map/ppermute | solution.py:37
  (377 shorter events, 73.9 us)
Async XLA Ops:
  7.2 66.9 %all-gather.4.cloned.1.call-start = ((), (), s32[]{:S(2)}) async-start(), calls=%async_computation.3 | async-start | bytes 1966080 | tf_op jit(solution)/shard_map/all_gather | solution.py:41
  9.1 118.7 %all-gather.6.cloned.1.call-start = ((), (), s32[]{:S(2)}) async-start(), calls=%async_computation.4 | async-start | bytes 3276800 | tf_op jit(solution)/shard_map/all_gather | solution.py:41
  9.1 62.6 %copy-start.52 = (bf16[256,256]{1,0:T(8,128)(2,1)S(1)}, bf16[256,256]{1,0:T(8,128)(2,1)}, u32[]{:S(2)}) copy-start(bf16[256,256]{1,0:T(8,128)(2,1)} %param.23) | copy-start | bytes 393220
  10.4 6.1 %collective-permute-start.3 = (bf16[256,256]{1,0:T(8,128)(2,1)S(1)}, bf16[256,256]{1,0:T(8,128)(2,1)S(1)}, u32[]{:S(2)}, u32[]{:S(2)}) collective-permute-start(bf16[256,256]{1,0:T(8,128)(2,1)S(1)} %get-tuple-element.131), channel_id=1, source_target_pairs={{0,12},{1,8},{2,4},{3,0},{4,13},{5,9},{6,5},{7,1},{8,14},{9,10},{1... | collective-permute-start | bytes 393224 | tf_op jit(solution)/shard_map/ppermute | solution.py:91
  10.5 10.8 %collective-permute-start = (bf16[256,256]{1,0:T(8,128)(2,1)S(1)}, bf16[256,256]{1,0:T(8,128)(2,1)S(1)}, u32[]{:S(2)}, u32[]{:S(2)}) collective-permute-start(bf16[256,256]{1,0:T(8,128)(2,1)S(1)} %get-tuple-element.130), channel_id=1, source_target_pairs={{0,0},{1,4},{2,8},{3,12},{4,1},{5,5},{6,9},{7,13},{8,2},{9,6},{10,... | collective-permute-start | bytes 393224 | tf_op jit(solution)/shard_map/ppermute | solution.py:91
  16.4 39.6 %collective-permute-start.1 = (bf16[256,256]{1,0:T(8,128)(2,1)S(1)}, bf16[256,256]{1,0:T(8,128)(2,1)S(1)}, u32[]{:S(2)}, u32[]{:S(2)}) collective-permute-start(bf16[256,256]{1,0:T(8,128)(2,1)S(1)} %get-tuple-element.133), channel_id=1, source_target_pairs={{0,4},{1,0},{2,12},{3,8},{4,5},{5,1},{6,13},{7,9},{8,6},{9,2},{10,... | collective-permute-start | bytes 393224 | tf_op jit(solution)/shard_map/ppermute | solution.py:91
  16.4 39.5 %collective-permute-start.2 = (bf16[256,256]{1,0:T(8,128)(2,1)S(1)}, bf16[256,256]{1,0:T(8,128)(2,1)S(1)}, u32[]{:S(2)}, u32[]{:S(2)}) collective-permute-start(bf16[256,256]{1,0:T(8,128)(2,1)S(1)} %get-tuple-element.132), channel_id=1, source_target_pairs={{0,8},{1,12},{2,0},{3,4},{4,9},{5,13},{6,1},{7,5},{8,10},{9,14},{1... | collective-permute-start | bytes 393224 | tf_op jit(solution)/shard_map/ppermute | solution.py:91
  56.1 91.8 %copy-start.16 = (bf16[256,256]{1,0:T(8,128)(2,1)}, bf16[256,256]{1,0:T(8,128)(2,1)S(1)}, u32[]{:S(2)}) copy-start(bf16[256,256]{1,0:T(8,128)(2,1)S(1)} %get-tuple-element.126) | copy-start | bytes 393220
  56.1 91.8 %copy-start.18 = (bf16[256,256]{1,0:T(8,128)(2,1)}, bf16[256,256]{1,0:T(8,128)(2,1)S(1)}, u32[]{:S(2)}) copy-start(bf16[256,256]{1,0:T(8,128)(2,1)S(1)} %get-tuple-element.127) | copy-start | bytes 393220
  56.1 91.8 %copy-start.20 = (bf16[256,256]{1,0:T(8,128)(2,1)}, bf16[256,256]{1,0:T(8,128)(2,1)S(1)}, u32[]{:S(2)}) copy-start(bf16[256,256]{1,0:T(8,128)(2,1)S(1)} %get-tuple-element.128) | copy-start | bytes 393220
  56.1 91.8 %copy-start.22 = (bf16[256,256]{1,0:T(8,128)(2,1)}, bf16[256,256]{1,0:T(8,128)(2,1)S(1)}, u32[]{:S(2)}) copy-start(bf16[256,256]{1,0:T(8,128)(2,1)S(1)} %get-tuple-element.129) | copy-start | bytes 393220
  56.2 11.4 %collective-permute-start.4 = (bf16[256,1024]{1,0:T(8,128)(2,1)S(1)}, bf16[256,1024]{1,0:T(8,128)(2,1)S(1)}, u32[]{:S(2)}, u32[]{:S(2)}) collective-permute-start(bf16[256,1024]{1,0:T(8,128)(2,1)S(1)} %pad_maximum_fusion.16), channel_id=1, source_target_pairs={{0,8},{4,12},{8,0},{12,4},{1,9},{5,13},{9,1},{13,5},{2,10},{6,14},... | collective-permute-start | bytes 1572872 | tf_op jit(solution)/shard_map/ppermute | solution.py:37
  68.4 5.5 %collective-permute-start.5 = (bf16[512,1024]{1,0:T(8,128)(2,1)S(1)}, bf16[512,1024]{1,0:T(8,128)(2,1)S(1)}, u32[]{:S(2)}, u32[]{:S(2)}) collective-permute-start(bf16[512,1024]{1,0:T(8,128)(2,1)S(1)} %pad_maximum_fusion.5), channel_id=1, source_target_pairs={{0,4},{4,0},{8,12},{12,8},{1,5},{5,1},{9,13},{13,9},{2,6},{6,2},{1... | collective-permute-start | bytes 3145736 | tf_op jit(solution)/shard_map/ppermute | solution.py:37
  73.7 136.6 %all-gather.8.cloned.1.call-start = ((), (), s32[]{:S(2)}) async-start(), calls=%async_computation.5 | async-start | bytes 2621440 | tf_op jit(solution)/shard_map/all_gather | solution.py:41
  88.7 41.1 %copy-start.7 = (bf16[32,8,2,512]{3,1,2,0:T(8,128)(2,1)}, bf16[32,8,2,512]{3,1,2,0:T(8,128)(2,1)S(1)}, u32[]{:S(2)}) copy-start(bf16[32,8,2,512]{3,1,2,0:T(8,128)(2,1)S(1)} %copy.88) | copy-start | bytes 1572868
  129.9 2.7 collective-permute-start.6
  133.7 14.2 %collective-permute-start.7 = (bf16[256,1024]{1,0:T(8,128)(2,1)}, bf16[256,1024]{1,0:T(8,128)(2,1)S(1)}, u32[]{:S(2)}, u32[]{:S(2)}) collective-permute-start(bf16[256,1024]{1,0:T(8,128)(2,1)} %fusion.57), channel_id=1, source_target_pairs={{0,8},{4,12},{8,0},{12,4},{1,9},{5,13},{9,1},{13,5},{2,10},{6,14},... | collective-permute-start | bytes 1572872 | tf_op jit(solution)/shard_map/ppermute | solution.py:37
  135.5 4.5 collective-permute-start.8
  137.1 4.5 collective-permute-start.9
  138.8 5.4 %collective-permute-start.10 = (f32[6,256]{1,0:T(8,128)S(1)}, f32[6,256]{1,0:T(8,128)S(1)}, u32[]{:S(2)}, u32[]{:S(2)}) collective-permute-start(f32[6,256]{1,0:T(8,128)S(1)} %stack.172), channel_id=1, source_target_pairs={{0,3},{1,2},{2,1},{3,0},{4,7},{5,6},{6,5},{7,4},{8,11},{9,10},{10,... | collective-permute-start | bytes 18440 | tf_op jit(solution)/shard_map/ppermute | solution.py:37
  145.5 97.9 %copy-start.54 = (f32[1,1024]{1,0:T(1,128)}, f32[1,1024]{1,0:T(1,128)S(1)}, u32[]{:S(2)}) copy-start(f32[1,1024]{1,0:T(1,128)S(1)} %get-tuple-element.143) | copy-start | bytes 12292
  145.5 99.9 %copy-start.58 = (f32[1,1024]{1,0:T(1,128)}, f32[1,1024]{1,0:T(1,128)S(1)}, u32[]{:S(2)}) copy-start(f32[1,1024]{1,0:T(1,128)S(1)} %get-tuple-element.140) | copy-start | bytes 12292
  149.7 93.8 %copy-start.62 = (f32[256]{0:T(256)}, f32[256]{0:T(256)S(1)}, u32[]{:S(2)}) copy-start(f32[256]{0:T(256)S(1)} %broadcast_multiply_fusion.5) | copy-start | bytes 3076
  150.8 35.8 %copy-start.14 = (bf16[256,1024]{1,0:T(8,128)(2,1)}, bf16[256,1024]{1,0:T(8,128)(2,1)S(1)}, u32[]{:S(2)}) copy-start(bf16[256,1024]{1,0:T(8,128)(2,1)S(1)} %fusion.63) | copy-start | bytes 1572868
  150.8 13.2 %collective-permute-start.11 = (bf16[256,1024]{1,0:T(8,128)(2,1)S(1)}, bf16[256,1024]{1,0:T(8,128)(2,1)S(1)}, u32[]{:S(2)}, u32[]{:S(2)}) collective-permute-start(bf16[256,1024]{1,0:T(8,128)(2,1)S(1)} %fusion.63), channel_id=1, source_target_pairs={{0,8},{4,12},{8,0},{12,4},{1,9},{5,13},{9,1},{13,5},{2,10},{6,14},... | collective-permute-start | bytes 1572872 | tf_op jit(solution)/shard_map/ppermute | solution.py:37
  164.0 22.6 %copy-start.36 = (bf16[256,1024]{1,0:T(8,128)(2,1)}, bf16[256,1024]{1,0:T(8,128)(2,1)S(1)}, u32[]{:S(2)}) copy-start(bf16[256,1024]{1,0:T(8,128)(2,1)S(1)} %collective-permute-done.11) | copy-start | bytes 1572868
  165.2 3.0 collective-permute-start.12
  165.2 256.0 %reduce-scatter.8.cloned.1.call-start = ((), (), s32[]{:S(2)}) async-start(), calls=%async_computation.8 | async-start | bytes 2621440 | tf_op jit(solution)/shard_map/reduce_scatter | solution.py:123
  215.1 28.4 %copy-start.65 = (f32[256]{0:T(256)S(1)}, f32[256]{0:T(256)}, u32[]{:S(2)}) copy-start(f32[256]{0:T(256)} %copy-done.64) | copy-start | bytes 3076
  215.1 28.4 %copy-start.69 = (f32[1,1024]{1,0:T(1,128)S(1)}, f32[1,1024]{1,0:T(1,128)}, u32[]{:S(2)}) copy-start(f32[1,1024]{1,0:T(1,128)} %get-tuple-element.141) | copy-start | bytes 12292
  215.1 2.7 collective-permute-start.13
  218.0 25.4 %collective-permute-start.14 = (bf16[256,1024]{1,0:T(8,128)(2,1)S(1)}, bf16[256,1024]{1,0:T(8,128)(2,1)S(1)}, u32[]{:S(2)}, u32[]{:S(2)}) collective-permute-start(bf16[256,1024]{1,0:T(8,128)(2,1)S(1)} %fusion.53), channel_id=1, source_target_pairs={{0,8},{4,12},{8,0},{12,4},{1,9},{5,13},{9,1},{13,5},{2,10},{6,14},... | collective-permute-start | bytes 1572872 | tf_op jit(solution)/shard_map/ppermute | solution.py:37
  219.5 9.9 %collective-permute-start.19 = (bf16[256,256]{1,0:T(8,128)(2,1)S(1)}, bf16[256,256]{1,0:T(8,128)(2,1)S(1)}, u32[]{:S(2)}, u32[]{:S(2)}) collective-permute-start(bf16[256,256]{1,0:T(8,128)(2,1)S(1)} %get-tuple-element.106), channel_id=1, source_target_pairs={{0,0},{1,4},{2,8},{3,12},{4,1},{5,5},{6,9},{7,13},{8,2},{9,6},{10,... | collective-permute-start | bytes 393224 | tf_op jit(solution)/shard_map/ppermute | solution.py:91
  224.2 17.7 %collective-permute-start.20 = (bf16[256,256]{1,0:T(8,128)(2,1)S(1)}, bf16[256,256]{1,0:T(8,128)(2,1)S(1)}, u32[]{:S(2)}, u32[]{:S(2)}) collective-permute-start(bf16[256,256]{1,0:T(8,128)(2,1)S(1)} %get-tuple-element.109), channel_id=1, source_target_pairs={{0,4},{1,0},{2,12},{3,8},{4,5},{5,1},{6,13},{7,9},{8,6},{9,2},{10,... | collective-permute-start | bytes 393224 | tf_op jit(solution)/shard_map/ppermute | solution.py:91
  226.3 15.5 %collective-permute-start.21 = (bf16[256,256]{1,0:T(8,128)(2,1)S(1)}, bf16[256,256]{1,0:T(8,128)(2,1)S(1)}, u32[]{:S(2)}, u32[]{:S(2)}) collective-permute-start(bf16[256,256]{1,0:T(8,128)(2,1)S(1)} %get-tuple-element.108), channel_id=1, source_target_pairs={{0,8},{1,12},{2,0},{3,4},{4,9},{5,13},{6,1},{7,5},{8,10},{9,14},{1... | collective-permute-start | bytes 393224 | tf_op jit(solution)/shard_map/ppermute | solution.py:91
  226.3 16.9 %collective-permute-start.22 = (bf16[256,256]{1,0:T(8,128)(2,1)S(1)}, bf16[256,256]{1,0:T(8,128)(2,1)S(1)}, u32[]{:S(2)}, u32[]{:S(2)}) collective-permute-start(bf16[256,256]{1,0:T(8,128)(2,1)S(1)} %get-tuple-element.107), channel_id=1, source_target_pairs={{0,12},{1,8},{2,4},{3,0},{4,13},{5,9},{6,5},{7,1},{8,14},{9,10},{1... | collective-permute-start | bytes 393224 | tf_op jit(solution)/shard_map/ppermute | solution.py:91
  246.4 13.9 %collective-permute-start.23 = (bf16[256,1024]{1,0:T(8,128)(2,1)S(1)}, bf16[256,1024]{1,0:T(8,128)(2,1)S(1)}, u32[]{:S(2)}, u32[]{:S(2)}) collective-permute-start(bf16[256,1024]{1,0:T(8,128)(2,1)S(1)} %get-tuple-element.89), channel_id=1, source_target_pairs={{0,8},{4,12},{8,0},{12,4},{1,9},{5,13},{9,1},{13,5},{2,10},{6,14},... | collective-permute-start | bytes 1572872 | tf_op jit(solution)/shard_map/ppermute | solution.py:37
  260.3 2.7 collective-permute-start.24
  267.9 153.3 %reduce-scatter.6.cloned.1.call-start = ((), (), s32[]{:S(2)}) async-start(), calls=%async_computation.7 | async-start | bytes 2621440 | tf_op jit(solution)/shard_map/reduce_scatter | solution.py:123
  275.1 25.4 %copy-start.11 = (bf16[1024,1024]{1,0:T(8,128)(2,1)}, bf16[1024,1024]{1,0:T(8,128)(2,1)S(1)}, u32[]{:S(2)}) copy-start(bf16[1024,1024]{1,0:T(8,128)(2,1)S(1)} %fusion.12) | copy-start | bytes 6291460
  277.8 2.7 collective-permute-start.25
  280.7 14.1 %collective-permute-start.26 = (bf16[256,1024]{1,0:T(8,128)(2,1)S(1)}, bf16[256,1024]{1,0:T(8,128)(2,1)S(1)}, u32[]{:S(2)}, u32[]{:S(2)}) collective-permute-start(bf16[256,1024]{1,0:T(8,128)(2,1)S(1)} %fusion.50), channel_id=1, source_target_pairs={{0,8},{4,12},{8,0},{12,4},{1,9},{5,13},{9,1},{13,5},{2,10},{6,14},... | collective-permute-start | bytes 1572872 | tf_op jit(solution)/shard_map/ppermute | solution.py:37
  298.8 13.3 %collective-permute-start.27 = (bf16[256,1024]{1,0:T(8,128)(2,1)S(1)}, bf16[256,1024]{1,0:T(8,128)(2,1)S(1)}, u32[]{:S(2)}, u32[]{:S(2)}) collective-permute-start(bf16[256,1024]{1,0:T(8,128)(2,1)S(1)} %get-tuple-element.58), channel_id=1, source_target_pairs={{0,8},{4,12},{8,0},{12,4},{1,9},{5,13},{9,1},{13,5},{2,10},{6,14},... | collective-permute-start | bytes 1572872 | tf_op jit(solution)/shard_map/ppermute | solution.py:37
  313.1 4.4 collective-permute-start.28
  315.7 132.3 %reduce-scatter.4.cloned.1.call-start = ((), (), s32[]{:S(2)}) async-start(), calls=%async_computation.6 | async-start | bytes 2621440 | tf_op jit(solution)/shard_map/reduce_scatter | solution.py:123
  356.6 66.6 %copy-start.4 = (f32[256,1024]{1,0:T(8,128)S(1)}, f32[256,1024]{1,0:T(8,128)}, u32[]{:S(2)}) copy-start(f32[256,1024]{1,0:T(8,128)} %get-tuple-element.59) | copy-start | bytes 3145732
  356.6 47.5 %collective-permute-start.29 = (bf16[512,1024]{1,0:T(8,128)(2,1)}, bf16[512,1024]{1,0:T(8,128)(2,1)S(1)}, u32[]{:S(2)}, u32[]{:S(2)}) collective-permute-start(bf16[512,1024]{1,0:T(8,128)(2,1)} %pad_maximum_fusion.12), channel_id=1, source_target_pairs={{0,4},{4,0},{8,12},{12,8},{1,5},{5,1},{9,13},{13,9},{2,6},{6,2},{1... | collective-permute-start | bytes 3145736 | tf_op jit(solution)/shard_map/ppermute | solution.py:37
  357.8 5.4 %collective-permute-start.36 = (f32[7936]{0:T(1024)S(1)}, f32[7936]{0:T(1024)S(1)}, u32[]{:S(2)}, u32[]{:S(2)}) collective-permute-start(f32[7936]{0:T(1024)S(1)} %constant_dynamic-update-slice_fusion.4), channel_id=1, source_target_pairs={{0,1},{1,0},{2,3},{3,2},{4,5},{5,4},{6,7},{7,6},{8,9},{9,8},{10,11... | collective-permute-start | bytes 95240 | tf_op jit(solution)/shard_map/ppermute | solution.py:37
  363.2 7.2 %collective-permute-start.37 = (f32[7936]{0:T(1024)S(1)}, f32[7936]{0:T(1024)S(1)}, u32[]{:S(2)}, u32[]{:S(2)}) collective-permute-start(f32[7936]{0:T(1024)S(1)} %add.277), channel_id=1, source_target_pairs={{0,2},{1,3},{2,0},{3,1},{4,6},{5,7},{6,4},{7,5},{8,10},{9,11},{10,... | collective-permute-start | bytes 95240 | tf_op jit(solution)/shard_map/ppermute | solution.py:37
  365.8 12.9 %collective-permute-start.15 = (bf16[256,256]{1,0:T(8,128)(2,1)S(1)}, bf16[256,256]{1,0:T(8,128)(2,1)S(1)}, u32[]{:S(2)}, u32[]{:S(2)}) collective-permute-start(bf16[256,256]{1,0:T(8,128)(2,1)S(1)} %get-tuple-element.118), channel_id=1, source_target_pairs={{0,0},{1,4},{2,8},{3,12},{4,1},{5,5},{6,9},{7,13},{8,2},{9,6},{10,... | collective-permute-start | bytes 393224 | tf_op jit(solution)/shard_map/ppermute | solution.py:103
  367.9 17.5 %collective-permute-start.16 = (bf16[256,256]{1,0:T(8,128)(2,1)S(1)}, bf16[256,256]{1,0:T(8,128)(2,1)S(1)}, u32[]{:S(2)}, u32[]{:S(2)}) collective-permute-start(bf16[256,256]{1,0:T(8,128)(2,1)S(1)} %get-tuple-element.121), channel_id=1, source_target_pairs={{0,1},{1,5},{2,9},{3,13},{4,0},{5,4},{6,8},{7,12},{8,3},{9,7},{10,... | collective-permute-start | bytes 393224 | tf_op jit(solution)/shard_map/ppermute | solution.py:103
  370.4 15.0 %collective-permute-start.17 = (bf16[256,256]{1,0:T(8,128)(2,1)S(1)}, bf16[256,256]{1,0:T(8,128)(2,1)S(1)}, u32[]{:S(2)}, u32[]{:S(2)}) collective-permute-start(bf16[256,256]{1,0:T(8,128)(2,1)S(1)} %get-tuple-element.120), channel_id=1, source_target_pairs={{0,2},{1,6},{2,10},{3,14},{4,3},{5,7},{6,11},{7,15},{8,0},{9,4},{1... | collective-permute-start | bytes 393224 | tf_op jit(solution)/shard_map/ppermute | solution.py:103
  370.4 17.6 %collective-permute-start.18 = (bf16[256,256]{1,0:T(8,128)(2,1)S(1)}, bf16[256,256]{1,0:T(8,128)(2,1)S(1)}, u32[]{:S(2)}, u32[]{:S(2)}) collective-permute-start(bf16[256,256]{1,0:T(8,128)(2,1)S(1)} %get-tuple-element.119), channel_id=1, source_target_pairs={{0,3},{1,7},{2,11},{3,15},{4,2},{5,6},{6,10},{7,14},{8,1},{9,5},{1... | collective-permute-start | bytes 393224 | tf_op jit(solution)/shard_map/ppermute | solution.py:103
  378.7 9.4 %collective-permute-start.38 = (f32[7936]{0:T(1024)S(1)}, f32[7936]{0:T(1024)S(1)}, u32[]{:S(2)}, u32[]{:S(2)}) collective-permute-start(f32[7936]{0:T(1024)S(1)} %add.278), channel_id=1, source_target_pairs={{0,16},{16,0},{1,17},{17,1},{2,18},{18,2},{3,19},{19,3},{4,20},{20... | collective-permute-start | bytes 95240 | tf_op jit(solution)/shard_map/ppermute | solution.py:37
  388.2 18.1 %collective-permute-start.39 = (f32[6,256]{1,0:T(8,128)S(1)}, f32[6,256]{1,0:T(8,128)S(1)}, u32[]{:S(2)}, u32[]{:S(2)}) collective-permute-start(f32[6,256]{1,0:T(8,128)S(1)} %constant_dynamic-slice_fusion), channel_id=1, source_target_pairs={{0,4},{4,0},{8,12},{12,8},{1,5},{5,1},{9,13},{13,9},{2,6},{6,2},{1... | collective-permute-start | bytes 18440 | tf_op jit(solution)/shard_map/ppermute | solution.py:37
  406.3 16.9 %collective-permute-start.30 = (bf16[256,1024]{1,0:T(8,128)(2,1)}, bf16[256,1024]{1,0:T(8,128)(2,1)S(1)}, u32[]{:S(2)}, u32[]{:S(2)}) collective-permute-start(bf16[256,1024]{1,0:T(8,128)(2,1)} %fusion.46), channel_id=1, source_target_pairs={{0,8},{4,12},{8,0},{12,4},{1,9},{5,13},{9,1},{13,5},{2,10},{6,14},... | collective-permute-start | bytes 1572872 | tf_op jit(solution)/shard_map/ppermute | solution.py:37
  406.3 14.2 %collective-permute-start.40 = (f32[6,256]{1,0:T(8,128)S(1)}, f32[6,256]{1,0:T(8,128)S(1)}, u32[]{:S(2)}, u32[]{:S(2)}) collective-permute-start(f32[6,256]{1,0:T(8,128)S(1)} %fusion.138), channel_id=1, source_target_pairs={{0,8},{4,12},{8,0},{12,4},{1,9},{5,13},{9,1},{13,5},{2,10},{6,14},... | collective-permute-start | bytes 18440 | tf_op jit(solution)/shard_map/ppermute | solution.py:37
  421.1 15.2 %collective-permute-start.42 = (bf16[256,1024]{1,0:T(8,128)(2,1)}, bf16[256,1024]{1,0:T(8,128)(2,1)}, u32[]{:S(2)}, u32[]{:S(2)}) collective-permute-start(bf16[256,1024]{1,0:T(8,128)(2,1)} %reduce-scatter.8.cloned.1.call-done), channel_id=1, source_target_pairs={{0,16},{16,0},{1,17},{17,1},{2,18},{18,2},{3,19},{19,3},{4,20},{20... | collective-permute-start | bytes 1572872 | tf_op jit(solution)/shard_map/ppermute | solution.py:37
  421.2 24.4 %collective-permute-start.41 = (bf16[256,1024]{1,0:T(8,128)(2,1)}, bf16[256,1024]{1,0:T(8,128)(2,1)S(1)}, u32[]{:S(2)}, u32[]{:S(2)}) collective-permute-start(bf16[256,1024]{1,0:T(8,128)(2,1)} %reduce-scatter.6.cloned.1.call-done), channel_id=1, source_target_pairs={{0,16},{16,0},{1,17},{17,1},{2,18},{18,2},{3,19},{19,3},{4,20},{20... | collective-permute-start | bytes 1572872 | tf_op jit(solution)/shard_map/ppermute | solution.py:37
  424.9 23.4 %collective-permute-start.31 = (bf16[256,256]{1,0:T(8,128)(2,1)S(1)}, bf16[256,256]{1,0:T(8,128)(2,1)S(1)}, u32[]{:S(2)}, u32[]{:S(2)}) collective-permute-start(bf16[256,256]{1,0:T(8,128)(2,1)S(1)} %get-tuple-element.94), channel_id=1, source_target_pairs={{0,0},{1,4},{2,8},{3,12},{4,1},{5,5},{6,9},{7,13},{8,2},{9,6},{10,... | collective-permute-start | bytes 393224 | tf_op jit(solution)/shard_map/ppermute | solution.py:103
  426.9 21.5 %collective-permute-start.32 = (bf16[256,256]{1,0:T(8,128)(2,1)S(1)}, bf16[256,256]{1,0:T(8,128)(2,1)S(1)}, u32[]{:S(2)}, u32[]{:S(2)}) collective-permute-start(bf16[256,256]{1,0:T(8,128)(2,1)S(1)} %get-tuple-element.97), channel_id=1, source_target_pairs={{0,1},{1,5},{2,9},{3,13},{4,0},{5,4},{6,8},{7,12},{8,3},{9,7},{10,... | collective-permute-start | bytes 393224 | tf_op jit(solution)/shard_map/ppermute | solution.py:103
  428.7 19.7 %collective-permute-start.33 = (bf16[256,256]{1,0:T(8,128)(2,1)S(1)}, bf16[256,256]{1,0:T(8,128)(2,1)S(1)}, u32[]{:S(2)}, u32[]{:S(2)}) collective-permute-start(bf16[256,256]{1,0:T(8,128)(2,1)S(1)} %get-tuple-element.96), channel_id=1, source_target_pairs={{0,2},{1,6},{2,10},{3,14},{4,3},{5,7},{6,11},{7,15},{8,0},{9,4},{1... | collective-permute-start | bytes 393224 | tf_op jit(solution)/shard_map/ppermute | solution.py:103
  436.3 12.0 %collective-permute-start.34 = (bf16[256,256]{1,0:T(8,128)(2,1)S(1)}, bf16[256,256]{1,0:T(8,128)(2,1)S(1)}, u32[]{:S(2)}, u32[]{:S(2)}) collective-permute-start(bf16[256,256]{1,0:T(8,128)(2,1)S(1)} %get-tuple-element.95), channel_id=1, source_target_pairs={{0,3},{1,7},{2,11},{3,15},{4,2},{5,6},{6,10},{7,14},{8,1},{9,5},{1... | collective-permute-start | bytes 393224 | tf_op jit(solution)/shard_map/ppermute | solution.py:103
  448.0 12.3 %collective-permute-start.35 = (bf16[256,1024]{0,1:T(8,128)(2,1)}, bf16[256,1024]{0,1:T(8,128)(2,1)S(1)}, u32[]{:S(2)}, u32[]{:S(2)}) collective-permute-start(bf16[256,1024]{0,1:T(8,128)(2,1)} %reduce-scatter.4.cloned.1.call-done), channel_id=1, source_target_pairs={{0,16},{16,0},{1,17},{17,1},{2,18},{18,2},{3,19},{19,3},{4,20},{20... | collective-permute-start | bytes 1572872 | tf_op jit(solution)/shard_map/ppermute | solution.py:37
  (82 other events, 576.4 us)
Sparse Core Ops, SparseCore 0:
  10.2 42.0 all-gather.3
  73.9 53.8 all-gather.5
  165.3 45.0 all-gather.7
  268.0 43.5 reduce-scatter.7
  315.8 43.7 reduce-scatter.5
  361.8 51.5 reduce-scatter.3
